TPU v7x, 128 devices: a whole 4x4x4 slice. The times are simulated.
128 devices in a mesh: along: 4 (over x_lo, core), cross: 32 (over z, x_hi, y).
Axes of the slice: x: 4 (x_hi: 2, x_lo: 2; x = x_hi * 2 + x_lo), y: 4, z: 4, core: 2. Of those that a mesh axis runs over, the one named last changes fastest.
Arguments:
- adjoint_state: float32 [4, 32, 128, 4, 512], P(None, 'along', 'cross'), may hold values from -6 to 6
- snapshot_store: float32 [8192, 3, 4, 512], P(('along', 'cross')), may hold values from -6 to 6
- dispatch_slot: int32 [8192], P(('along', 'cross')), may hold values from 0 to 63, as said below
- arrival_slot: int32 [32, 128], P('along', 'cross'), may hold values from -1 to 63, as said below
- mic_node: int32 [16384], P(('along', 'cross')), may hold values from 0 to 2047
- mic_residual: float32 [16384], P(('along', 'cross')), may hold values from -6 to 6
Outputs:
- adjoint_next: float32 [4, 32, 128, 4, 512], P(None, 'along', 'cross')
- kappa_gradient: float32 [32, 128, 4, 512], P('along', 'cross')
Inputs may be any that keep to these rules, and one draw needn't show every extreme that they name: `dispatch_slot`: each device's 64 entries are a permutation of 0 to 63. `arrival_slot`: on each device exactly 16 of the 8 x 4 columns are active; their values are distinct positions h * 2 + s (h a cross index, s < 2); the others are -1. Some holder fills all 2 slots to each owner.
All inputs are finite; a program needn't handle non-finite values.
Results may differ from a plain program's by a relative error of at most 0.00007.
Values sent between devices are 32-bit elements; how exact they have to be, the bound alone decides.
No kernel may reach another device: no remote copies, remote signals or barrier semaphores. Data moves between devices by JAX's collectives and lax.ppermute only.
A program may use at most 256 MiB of HBM per device.

v0:
```python
import jax
import jax.numpy as jnp
import numpy as np
from jax import lax
from jax.sharding import PartitionSpec as P

MACH = 0.3
ALPHA = 1.3
LIFT_SCALE = 56.0
TIME_STEP = 0.004
SOURCE_GAIN = 50.0
PRECISE = lax.Precision.HIGHEST
LOBATTO_INNER = [
    -0.8717401485096066,
    -0.5917001814331423,
    -0.2092992179024789,
    0.2092992179024789,
    0.5917001814331423,
    0.8717401485096066,
]


def with_halo(shard, sides, width):
    for axis, dim in sides:
        peers, length = (lax.axis_size(axis), shard.shape[dim])
        up = [(i, (i + 1) % peers) for i in range(peers - 1)]
        down = [(j, i) for i, j in up]
        last = lax.slice_in_dim(shard, length - width, length, axis=dim)
        first = lax.slice_in_dim(shard, 0, width, axis=dim)
        before = lax.ppermute(last, axis, up)
        after = lax.ppermute(first, axis, down)
        shard = jnp.concatenate([before, shard, after], axis=dim)
    return shard


def legendre_seven(points):
    previous = points * 0.0 + 1.0
    current = points * 1.0
    for degree_index in range(1, 7):
        following = ((2 * degree_index + 1) * points * current - degree_index * previous) / (
            degree_index + 1
        )
        previous, current = (current, following)
    return current


def derivative_tables():
    degree = 7
    points = np.array([-1.0] + LOBATTO_INNER + [1.0])
    values = legendre_seven(points)
    differ = points[:, None] - points[None, :] + np.eye(degree + 1)
    matrix = values[:, None] / values[None, :] / differ
    matrix = matrix * (1.0 - np.eye(degree + 1))
    matrix[0, 0] = -degree * (degree + 1) / 4.0
    matrix[degree, degree] = degree * (degree + 1) / 4.0
    identity_8 = np.eye(8)
    identity_64 = np.eye(64)
    along_table = 2.0 * np.kron(matrix, identity_64)
    cross_table = 2.0 * np.kron(np.kron(identity_8, matrix), identity_8)
    vertical_table = 2.0 * np.kron(identity_64, matrix)
    return tuple(
        (
            jnp.asarray(operator_table.T, dtype=jnp.float32)
            for operator_table in (along_table, cross_table, vertical_table)
        )
    )


def derivative(nodal_rows, operator_table):
    flat_rows = nodal_rows.reshape(-1, 512)
    return jnp.dot(flat_rows, operator_table, precision=PRECISE).reshape(nodal_rows.shape)


def volume_terms(adjoint, tables):
    slope_along = derivative(adjoint, tables[0])
    slope_cross = derivative(jnp.stack([adjoint[0], adjoint[2]]), tables[1])
    slope_vertical = derivative(jnp.stack([adjoint[0], adjoint[3]]), tables[2])
    return jnp.stack(
        [
            MACH * slope_along[0] + slope_along[1] + slope_cross[1] + slope_vertical[1],
            MACH * slope_along[1] + slope_along[0],
            MACH * slope_along[2] + slope_cross[0],
            MACH * slope_along[3] + slope_vertical[0],
        ]
    )


def face_traces(adjoint):
    nodal = adjoint.reshape(adjoint.shape[:-1] + (8, 8, 8))
    return (
        nodal[..., 0, :, :],
        nodal[..., 7, :, :],
        nodal[..., :, 0, :],
        nodal[..., :, 7, :],
        nodal[..., :, :, 0],
        nodal[..., :, :, 7],
    )


def jump_flux(difference, direction, sign):
    pressure = difference[0]
    along_vel = difference[1]
    cross_vel = difference[2]
    vertical_vel = difference[3]
    nothing = jnp.zeros_like(pressure)
    if direction == 0:
        normal = [
            MACH * pressure + along_vel,
            MACH * along_vel + pressure,
            MACH * cross_vel,
            MACH * vertical_vel,
        ]
    elif direction == 1:
        normal = [cross_vel, nothing, pressure, nothing]
    else:
        normal = [vertical_vel, nothing, nothing, pressure]
    return -0.5 * LIFT_SCALE * (sign * jnp.stack(normal) + ALPHA * difference)


def vertical_exteriors(bottom, upper):
    mirror = jnp.array([1.0, 1.0, 1.0, -1.0], dtype=jnp.float32).reshape(4, 1, 1, 1, 1, 1)
    beneath = jnp.concatenate([bottom[:, :, :, :1] * mirror, upper[:, :, :, :-1]], axis=3)
    overhead = jnp.concatenate([bottom[:, :, :, 1:], jnp.zeros_like(bottom[:, :, :, :1])], axis=3)
    return (beneath, overhead)


def adjoint_rate(adjoint, tables, outside):
    inside = face_traces(adjoint)
    tendency = volume_terms(adjoint, tables)
    nodal = tendency.reshape(adjoint.shape[:-1] + (8, 8, 8))
    nodal = nodal.at[..., 0, :, :].add(jump_flux(inside[0] - outside[0], 0, -1.0))
    nodal = nodal.at[..., 7, :, :].add(jump_flux(inside[1] - outside[1], 0, 1.0))
    nodal = nodal.at[..., :, 0, :].add(jump_flux(inside[2] - outside[2], 1, -1.0))
    nodal = nodal.at[..., :, 7, :].add(jump_flux(inside[3] - outside[3], 1, 1.0))
    nodal = nodal.at[..., :, :, 0].add(jump_flux(inside[4] - outside[4], 2, -1.0))
    nodal = nodal.at[..., :, :, 7].add(jump_flux(inside[5] - outside[5], 2, 1.0))
    return nodal.reshape(adjoint.shape)


def divergence(fields, tables):
    return (
        derivative(fields[:, 0], tables[0])
        + derivative(fields[:, 1], tables[1])
        + derivative(fields[:, 2], tables[2])
    )


def ground_sources(node_index, values, total_nodes):
    return jnp.zeros((total_nodes,), jnp.float32).at[node_index].add(values)


def per_device(adjoint_state, snapshot_store, dispatch_slot, arrival_slot, mic_node, mic_residual):
    tables = derivative_tables()
    along_cells = adjoint_state.shape[1]
    cross_cells = adjoint_state.shape[2]
    layers = adjoint_state.shape[3]
    traces = face_traces(adjoint_state)
    along_stack = jnp.stack([traces[0], traces[1]]).reshape(
        2, 4, along_cells, cross_cells, layers * 64
    )
    along_padded = with_halo(along_stack, (("along", 2),), 1)
    along_padded = along_padded.reshape(2, 4, along_cells + 2, cross_cells, layers, 8, 8)
    cross_stack = jnp.stack([traces[2], traces[3]]).reshape(
        2, 4, along_cells, cross_cells, layers * 64
    )
    cross_padded = with_halo(cross_stack, (("cross", 3),), 1)
    cross_padded = cross_padded.reshape(2, 4, along_cells, cross_cells + 2, layers, 8, 8)
    lower_along = along_padded[1, :, :along_cells]
    upper_along = along_padded[0, :, 2:]
    lower_cross = cross_padded[1, :, :, :cross_cells]
    upper_cross = cross_padded[0, :, :, 2:]
    beneath, overhead = vertical_exteriors(traces[4], traces[5])
    outside = (lower_along, upper_along, lower_cross, upper_cross, beneath, overhead)
    updated = adjoint_state + TIME_STEP * adjoint_rate(adjoint_state, tables, outside)
    columns = along_cells * cross_cells
    sources = ground_sources(mic_node, mic_residual, columns * 64).reshape(
        along_cells, cross_cells, 64
    )
    updated = updated.at[0, :, :, 0, 0::8].add(TIME_STEP * SOURCE_GAIN * sources)
    cross_count = lax.axis_size("cross")
    slot_count = dispatch_slot.shape[0]
    capacity = slot_count // cross_count
    arrival = arrival_slot.reshape(columns)
    clipped = jnp.maximum(arrival, 0)
    active = (arrival >= 0).astype(jnp.float32).reshape(columns, 1, 1)
    multiplier = adjoint_state[0].reshape(columns, layers, 512)
    outgoing = snapshot_store[dispatch_slot].reshape(cross_count, capacity, 3, layers, 512)
    received = lax.all_to_all(outgoing, "cross", split_axis=0, concat_axis=0, tiled=True).reshape(
        slot_count, 3, layers, 512
    )
    spread = divergence(received[clipped], tables)
    gradient = TIME_STEP * multiplier * spread * active
    return (updated, gradient.reshape(along_cells, cross_cells, layers, 512))


def solution(mesh):
    in_specs = (
        P(None, "along", "cross", None, None),
        P(("along", "cross"), None, None, None),
        P(("along", "cross")),
        P("along", "cross"),
        P(("along", "cross")),
        P(("along", "cross")),
    )
    out_specs = (P(None, "along", "cross", None, None), P("along", "cross", None, None))
    return jax.shard_map(
        per_device, mesh=mesh, in_specs=in_specs, out_specs=out_specs, check_vma=False
    )
```

profile of v0, /device:TPU:32, one launch (start us, length us, event | category | flops | bytes accessed | tf_op | source)
XLA Modules:
  0.0 994.7 jit_solution(6786808318936369825)
XLA Ops:
  2.6 11.2 %reshape.634 = f32[4,8,4,4,8,8,8]{6,5,4,1,3,2,0:T(8,128)} reshape(f32[4,8,4,4,512]{4,1,3,2,0:T(8,128)S(1)} %copy.560) | data formatting | bytes 2097152 | tf_op jit(solution)/shard_map/reshape | solution.py:89
  34.1 15.9 %fusion.32 = (f32[4,8,4,4,8,1,8]{6,5,4,1,3,2,0:T(1,128)}, f32[4,8,4,4,8,1,8]{6,5,4,1,3,2,0:T(1,128)S(1)}) fusion(f32[4,8,4,4,8,8,8]{6,5,4,1,3,2,0:T(8,128)} %reshape.634), kind=kLoop, calls=%fused_computation.107 | loop fusion | bytes 524288 | tf_op jit(solution)/shard_map/slice | solution.py:94
  66.0 6.9 collective-permute-start.3
  75.5 7.7 all-to-all-start
  84.6 24.2 %fusion.31 = (f32[4,8,4,4,8,8,1]{6,5,4,1,3,2,0:T(8,128)}, f32[4,8,4,4,8,8,1]{6,5,4,1,3,2,0:T(8,128)}) fusion(f32[4,8,4,4,8,8,8]{6,5,4,1,3,2,0:T(8,128)} %reshape.634), kind=kLoop, calls=%fused_computation.106 | loop fusion | bytes 524288 | tf_op jit(solution)/shard_map/slice | solution.py:95
  155.0 26.7 %copy.622 = f32[4,8,4,4,8,8,1]{5,4,6,3,2,1,0:T(8,128)} copy(f32[4,8,4,4,8,8,1]{6,5,4,1,3,2,0:T(8,128)} %get-tuple-element.98) | data formatting | bytes 262144
  185.2 26.7 %copy.585 = f32[4,8,4,4,8,8,1]{5,4,3,2,1,0,6:T(8,128)} copy(f32[4,8,4,4,8,8,1]{6,5,4,1,3,2,0:T(8,128)} %get-tuple-element.99) | data formatting | bytes 262144 | tf_op jit(solution)/shard_map/slice | solution.py:96
  244.7 11.3 %copy.595 = f32[4,8,4,4,512]{1,2,4,3,0:T(4,128)} copy(f32[4,8,4,4,512]{4,3,2,1,0:T(4,128)S(1)} %copy-done.16) | data formatting | bytes 2097152 | tf_op args[0]
  256.0 26.5 %copy.591 = f32[4,8,4,4,8,8,1]{6,4,5,3,2,1,0:T(8,128)} copy(f32[4,8,4,4,8,8,1]{5,4,6,3,2,1,0:T(8,128)} %maximum_multiply_fusion.1) | data formatting | bytes 262144 | tf_op jit(solution)/shard_map/mul | solution.py:117
  282.6 26.6 %copy.592 = f32[4,8,4,4,8,8,1]{6,4,5,3,2,1,0:T(8,128)} copy(f32[4,8,4,4,8,8,1]{5,4,6,3,2,1,0:T(8,128)} %fusion.14) | data formatting | bytes 262144 | tf_op jit(solution)/shard_map/mul | solution.py:117
  309.1 26.6 %copy.593 = f32[4,8,4,4,8,8,1]{6,4,5,3,2,1,0:T(8,128)} copy(f32[4,8,4,4,8,8,1]{5,4,3,2,1,0,6:T(8,128)} %fusion.16) | data formatting | bytes 262144 | tf_op jit(solution)/shard_map/reshape.289
  352.0 9.4 slice_add_fusion.3
  361.4 54.7 %scatter-add.34 = f32[4,8,4,4,8,8,8]{6,4,5,3,2,1,0:T(8,128)} dynamic-update-slice(f32[4,8,4,4,8,8,8]{6,4,5,3,2,1,0:T(8,128)} %pad_maximum_fusion, f32[4,8,4,4,1,8,8]{6,4,5,3,2,1,0:T(1,128)} %slice_add_fusion.3, s32[]{:T(128)} %constant.188.clone.1, s32[]{:T(128)} %constant.188.clone.1, s32[]{:T(128)} %constant.188.clone.1, s32[]{:T(128)} %constant.188.clone.1, s32[]{:T(128)} %constant.188.clone.1, ...) | dynamic-update-slice | bytes 262148 | tf_op jit(solution)/shard_map/scatter-add | solution.py:131
  416.1 9.7 slice_add_fusion.2
  425.8 54.7 %scatter-add.35 = f32[4,8,4,4,8,8,8]{6,4,5,3,2,1,0:T(8,128)} dynamic-update-slice(f32[4,8,4,4,8,8,8]{6,4,5,3,2,1,0:T(8,128)} %scatter-add.34, f32[4,8,4,4,1,8,8]{6,4,5,3,2,1,0:T(1,128)} %slice_add_fusion.2, s32[]{:T(128)} %constant.188.clone.1, s32[]{:T(128)} %constant.188.clone.1, s32[]{:T(128)} %constant.188.clone.1, s32[]{:T(128)} %constant.188.clone.1, s32[]{:T(128)} %constant.189.clone.1, ...) | dynamic-update-slice | bytes 262148 | tf_op jit(solution)/shard_map/scatter-add | solution.py:132
  498.4 17.5 %slice_add_fusion.1 = f32[4,8,4,4,8,8,1]{6,4,5,3,2,1,0:T(8,128)} fusion(f32[4,8,4,4,8,8,8]{6,4,5,3,2,1,0:T(8,128)} %fusion.12, f32[4,8,4,4,8,8,1]{6,4,5,3,2,1,0:T(8,128)S(1)} %bitcast.170, f32[4,8,4,4,8,8,1]{6,4,5,3,2,1,0:T(8,128)} %copy.592), kind=kLoop, calls=%fused_computation.5 | loop fusion | flops 98304 | bytes 524288 | tf_op jit(solution)/shard_map/add | solution.py:135
  515.9 54.9 %scatter-add.48 = f32[4,8,4,4,8,8,8]{6,4,5,3,2,1,0:T(8,128)} dynamic-update-slice(f32[4,8,4,4,8,8,8]{6,4,5,3,2,1,0:T(8,128)} %fusion.12, f32[4,8,4,4,8,8,1]{6,4,5,3,2,1,0:T(8,128)} %slice_add_fusion.1, s32[]{:T(128)} %constant.188.clone.1, s32[]{:T(128)} %constant.188.clone.1, s32[]{:T(128)} %constant.188.clone.1, s32[]{:T(128)} %constant.188.clone.1, s32[]{:T(128)} %constant.188.clone.1, ...) | dynamic-update-slice | bytes 262148 | tf_op jit(solution)/shard_map/scatter-add | solution.py:135
  570.7 16.9 %slice_add_fusion = f32[4,8,4,4,8,8,1]{6,4,5,3,2,1,0:T(8,128)} fusion(f32[4,8,4,4,8,8,1]{6,4,5,3,2,1,0:T(8,128)} %copy.593, f32[4,8,4,4,8,8,8]{6,4,5,3,2,1,0:T(8,128)} %scatter-add.48), kind=kLoop, calls=%fused_computation.4 | loop fusion | flops 32768 | bytes 393216 | tf_op jit(solution)/shard_map/add | solution.py:136
  587.7 326.3 %scatter-add.49 = f32[4,8,4,4,8,8,8]{6,4,5,3,2,1,0:T(8,128)} dynamic-update-slice(f32[4,8,4,4,8,8,8]{6,4,5,3,2,1,0:T(8,128)} %scatter-add.48, f32[4,8,4,4,8,8,1]{6,4,5,3,2,1,0:T(8,128)} %slice_add_fusion, s32[]{:T(128)} %constant.188.clone.1, s32[]{:T(128)} %constant.188.clone.1, s32[]{:T(128)} %constant.188.clone.1, s32[]{:T(128)} %constant.188.clone.1, s32[]{:T(128)} %constant.188.clone.1, ...) | dynamic-update-slice | bytes 262148 | tf_op jit(solution)/shard_map/scatter-add | solution.py:136
  913.9 12.7 %broadcast_multiply_fusion = f32[4,8,4,4,8,8,8]{6,4,5,3,2,1,0:T(8,128)} fusion(f32[4,8,4,4,8,8,8]{6,4,5,3,2,1,0:T(8,128)} %scatter-add.49), kind=kLoop, calls=%fused_computation.7 | loop fusion | flops 262144 | bytes 2097152 | tf_op jit(solution)/shard_map/mul | solution.py:174
  926.6 20.8 %copy.610 = f32[4,8,4,4,8,8,8]{1,2,6,5,4,3,0:T(4,128)} copy(f32[4,8,4,4,8,8,8]{6,4,5,3,2,1,0:T(8,128)} %broadcast_multiply_fusion) | data formatting | bytes 2097152 | tf_op jit(solution)/shard_map/mul | solution.py:174
  947.4 18.4 %add.208 = f32[4,8,4,4,512]{1,2,4,3,0:T(4,128)} add(f32[4,8,4,4,512]{1,2,4,3,0:T(4,128)} %copy.595, f32[4,8,4,4,512]{1,2,4,3,0:T(4,128)} %bitcast.168) | non-fusion elementwise | flops 262144 | bytes 3145728 | tf_op jit(solution)/shard_map/add | solution.py:174
  965.8 6.9 scatter_fusion
  972.7 14.2 %copy.604 = f32[4,8,4,4,512]{4,3,2,1,0:T(4,128)} copy(f32[4,8,4,4,512]{1,2,4,3,0:T(4,128)} %scatter_fusion) | data formatting | bytes 2097152
  (184 shorter events, 165.5 us)
Async XLA Ops:
  0.6 72.3 %copy-start = (f32[64,3,4,512]{3,2,1,0:T(4,128)S(1)}, f32[64,3,4,512]{3,2,1,0:T(4,128)}, u32[]{:S(2)}) copy-start(f32[64,3,4,512]{3,2,1,0:T(4,128)} %param.23) | copy-start | bytes 4718596
  29.7 20.3 %copy-start.30 = (f32[2,4,8,4,256]{4,2,3,1,0:T(8,128)}, f32[2,4,8,4,256]{4,2,3,1,0:T(8,128)S(1)}, u32[]{:S(2)}) copy-start(f32[2,4,8,4,256]{4,2,3,1,0:T(8,128)S(1)} %copy_dynamic-update-slice_fusion.2) | copy-start | bytes 786436
  30.5 305.6 %collective-permute-start = (f32[2,4,1,4,256]{4,2,3,1,0:T(1,128)}, f32[2,4,1,4,256]{4,2,3,1,0:T(1,128)}, u32[]{:S(2)}, u32[]{:S(2)}) collective-permute-start(f32[2,4,1,4,256]{4,2,3,1,0:T(1,128)} %get-tuple-element.149), channel_id=1, source_target_pairs={{0,32},{32,64},{64,96},{1,33},{33,65},{65,97},{2,34},{34,66},{66,9... | collective-permute-start | bytes 98312 | tf_op jit(solution)/shard_map/ppermute | solution.py:30
  32.8 303.3 %collective-permute-start.1 = (f32[2,4,1,4,256]{4,2,3,1,0:T(1,128)}, f32[2,4,1,4,256]{4,2,3,1,0:T(1,128)}, u32[]{:S(2)}, u32[]{:S(2)}) collective-permute-start(f32[2,4,1,4,256]{4,2,3,1,0:T(1,128)} %get-tuple-element.150), channel_id=1, source_target_pairs={{32,0},{64,32},{96,64},{33,1},{65,33},{97,65},{34,2},{66,34},{98,6... | collective-permute-start | bytes 98312 | tf_op jit(solution)/shard_map/ppermute | solution.py:31
  59.0 13.9 %copy-start.34 = (s32[64]{0:T(128)S(1)}, s32[64]{0:T(128)}, u32[]{:S(2)}) copy-start(s32[64]{0:T(128)} %param.24) | copy-start | bytes 772
  61.8 13.7 %copy-start.26 = (f32[2,4,8,4,256]{4,2,3,1,0:T(8,128)}, f32[2,4,8,4,256]{4,2,3,1,0:T(8,128)S(1)}, u32[]{:S(2)}) copy-start(f32[2,4,8,4,256]{4,2,3,1,0:T(8,128)S(1)} %copy_dynamic-update-slice_fusion) | copy-start | bytes 786436
  62.5 418.1 %collective-permute-start.2 = (f32[2,4,8,1,256]{4,2,3,1,0:T(8,128)}, f32[2,4,8,1,256]{4,2,3,1,0:T(8,128)S(1)}, u32[]{:S(2)}, u32[]{:S(2)}) collective-permute-start(f32[2,4,8,1,256]{4,2,3,1,0:T(8,128)} %get-tuple-element.147), channel_id=1, source_target_pairs={{0,1},{1,2},{2,3},{3,4},{4,5},{5,6},{6,7},{7,8},{8,9},{9,10},{10,1... | collective-permute-start | bytes 196616 | tf_op jit(solution)/shard_map/ppermute | solution.py:30
  66.0 414.6 %collective-permute-start.3 = (f32[2,4,8,1,256]{4,2,3,1,0:T(8,128)}, f32[2,4,8,1,256]{4,2,3,1,0:T(8,128)S(1)}, u32[]{:S(2)}, u32[]{:S(2)}) collective-permute-start(f32[2,4,8,1,256]{4,2,3,1,0:T(8,128)} %get-tuple-element.148), channel_id=1, source_target_pairs={{1,0},{2,1},{3,2},{4,3},{5,4},{6,5},{7,6},{8,7},{9,8},{10,9},{11,1... | collective-permute-start | bytes 196616 | tf_op jit(solution)/shard_map/ppermute | solution.py:31
  75.5 7.7 copy-start.16
  75.5 911.4 %all-to-all-start = ((f32[32,2,3,4,512]{4,3,2,1,0:T(4,128)}), f32[32,2,3,4,512]{4,3,2,1,0:T(4,128)}, u32[]{:S(2)}, u32[]{:S(2)}) async-start(f32[32,2,3,4,512]{4,3,2,1,0:T(4,128)} %bitcast.52), calls=%async_computation | async-start | bytes 3145728 | tf_op jit(solution)/shard_map/all_to_all | solution.py:188
  84.6 24.3 %copy-start.32 = (s32[8,4]{0,1:T(4,128)S(1)}, s32[8,4]{0,1:T(4,128)}, u32[]{:S(2)}) copy-start(s32[8,4]{0,1:T(4,128)} %param.25) | copy-start | bytes 388
  84.6 24.3 %copy-start.22 = (f32[1,8,4,4,512]{4,3,2,1,0:T(4,128)S(1)}, f32[1,8,4,4,512]{4,3,2,1,0:T(4,128)}, u32[]{:S(2)}) copy-start(f32[1,8,4,4,512]{4,3,2,1,0:T(4,128)} %get-tuple-element.134) | copy-start | bytes 786436
  84.6 24.3 %copy-start.23 = (f32[1,8,4,4,512]{4,3,2,1,0:T(4,128)S(1)}, f32[1,8,4,4,512]{4,3,2,1,0:T(4,128)}, u32[]{:S(2)}) copy-start(f32[1,8,4,4,512]{4,3,2,1,0:T(4,128)} %get-tuple-element.135) | copy-start | bytes 786436
  222.3 6.6 copy-start.18
  222.3 9.8 copy-start.12
  225.9 6.3 copy-start.11
  232.2 6.3 copy-start.13
  309.1 27.0 %copy-start.31 = (f32[2,4,8,4,256]{4,2,3,1,0:T(8,128)S(1)}, f32[2,4,8,4,256]{4,2,3,1,0:T(8,128)}, u32[]{:S(2)}) copy-start(f32[2,4,8,4,256]{4,2,3,1,0:T(8,128)} %copy-done.30) | copy-start | bytes 786436
  341.5 7.1 copy-start.7
  341.5 7.1 copy-start.9
  425.8 54.8 %copy-start.27 = (f32[2,4,8,4,256]{4,2,3,1,0:T(8,128)S(1)}, f32[2,4,8,4,256]{4,2,3,1,0:T(8,128)}, u32[]{:S(2)}) copy-start(f32[2,4,8,4,256]{4,2,3,1,0:T(8,128)} %copy-done.26) | copy-start | bytes 786436
  489.1 9.2 slice-start
  489.2 9.2 slice-start.1
  490.1 8.2 slice-start.2
  (21 other events, 60.5 us)
where the time goes:
time: 1010 us; the launch traced here: 995 us
  local copies, waits for them, and re-layouts  820 us (81%)
  other arithmetic  138 us (14%)
  starting transfers between devices  21.7 us (2%)
  matrix products  13 us (1%)
    scatter-add x1, local copies, waits for them, and re-layouts, adjoint_rate(): nodal.at[..., :, :, 7].add(jump_flux(inside[5] - outside[5], 2, 1.0))  326 us
    unnamed x93, local copies, waits for them, and re-layouts  70.6 us
    scatter-add x1, local copies, waits for them, and re-layouts, adjoint_rate(): nodal.at[..., :, :, 0].add(jump_flux(inside[4] - outside[4], 2, -1.0))  54.9 us
    scatter-add x1, local copies, waits for them, and re-layouts, adjoint_rate(): nodal.at[..., 7, :, :].add(jump_flux(inside[1] - outside[1], 0, 1.0))  54.7 us
    scatter-add x1, local copies, waits for them, and re-layouts, adjoint_rate(): nodal.at[..., 0, :, :].add(jump_flux(inside[0] - outside[0], 0, -1.0))  54.7 us
    mul x2, local copies, waits for them, and re-layouts, jump_flux(): return -0.5 * LIFT_SCALE * (sign * jnp.stack(normal) + ALPHA * difference)  53.1 us
    another operation x2, local copies, waits for them, and re-layouts  28.7 us
    slice x1, local copies, waits for them, and re-layouts, face_traces(): nodal[..., :, :, 7]  26.7 us
  transfers between devices with their start and end apart: 5, of which 0 were waited for; matrix products, arithmetic and copies ran while one was open for 93% of the time, Pallas kernels for 0%

commit v1 on v0

v1 whole, which is shorter than its diff:
```python
import jax
import jax.numpy as jnp
import numpy as np
from jax import lax
from jax.experimental import pallas as pl
from jax.experimental.pallas import tpu as pltpu
from jax.sharding import PartitionSpec as P

MACH = 0.3
ALPHA = 1.3
LIFT_SCALE = 56.0
TIME_STEP = 0.004
SOURCE_GAIN = 50.0
HALF_LIFT = 0.5 * LIFT_SCALE
LOBATTO_INNER = [
    -0.8717401485096066,
    -0.5917001814331423,
    -0.2092992179024789,
    0.2092992179024789,
    0.5917001814331423,
    0.8717401485096066,
]
F32 = jnp.float32
BF16 = jnp.bfloat16
VMEM_BYTES = 24 * 1024 * 1024


def legendre_seven(points):
    previous = points * 0.0 + 1.0
    current = points * 1.0
    for degree_index in range(1, 7):
        following = ((2 * degree_index + 1) * points * current - degree_index * previous) / (
            degree_index + 1
        )
        previous, current = (current, following)
    return current


def high_low(table):
    table = table.astype(np.float32)
    high = table.astype(BF16)
    low = (table - high.astype(np.float32)).astype(BF16)
    return np.stack([high, low])


def derivative_tables():
    degree = 7
    points = np.array([-1.0] + LOBATTO_INNER + [1.0])
    values = legendre_seven(points)
    differ = points[:, None] - points[None, :] + np.eye(degree + 1)
    matrix = values[:, None] / values[None, :] / differ
    matrix = matrix * (1.0 - np.eye(degree + 1))
    matrix[0, 0] = -degree * (degree + 1) / 4.0
    matrix[degree, degree] = degree * (degree + 1) / 4.0
    along = 2.0 * np.kron(matrix, np.eye(64))
    cross = 2.0 * np.kron(np.kron(np.eye(4), matrix), np.eye(8))
    vertical = 2.0 * np.kron(np.eye(32), matrix)
    return high_low(along.T), high_low(np.concatenate([cross.T, vertical.T]))


def split(x):
    high = x.astype(BF16)
    return high, (x - high.astype(F32)).astype(BF16)


def product(high, low, table_high, table_low):
    def dot(a, b):
        return jnp.dot(a, b, preferred_element_type=F32)

    return dot(high, table_high) + (dot(low, table_high) + dot(high, table_low))


def lanes(shape):
    return lax.broadcasted_iota(jnp.int32, shape, len(shape) - 1)


def tile(t):
    return slice(128 * t, 128 * t + 128)


def holder_kernel(
    slot_ref, adj_ref, store_ref, gx_ref, gyz_ref,
    out_ref, last_along, first_along, last_cross, first_cross,
    stage, high, low,
):
    def gather(g, carry):
        rows = pl.ds(pl.multiple_of(g * 16, 16), 16)
        for m in range(4):
            slot = slot_ref[4 * g + m]
            for f in range(3):
                stage[f, g, 4 * m : 4 * m + 4, :] = store_ref[slot, f]
        for f in range(3):
            high[f, rows], low[f, rows] = split(stage[f, g])
        return carry

    lax.fori_loop(0, 16, gather, 0)
    for c in range(2):
        part = slice(256 * c, 256 * c + 256)
        total = product(high[0], low[0], gx_ref[0, :, part], gx_ref[1, :, part])
        for f in (1, 2):
            rows = slice(256 * (f - 1), 256 * f)
            total += product(high[f, :, part], low[f, :, part], gyz_ref[0, rows], gyz_ref[1, rows])
        out_ref[:, :, part] = total.reshape(32, 8, 256)
    for f in range(4):
        for c in range(4):
            last_along[f, 4 * c : 4 * c + 4, :] = adj_ref[f, 7, c, :, tile(3)]
            first_along[f, 4 * c : 4 * c + 4, :] = adj_ref[f, 0, c, :, tile(0)]
    j = (lanes((4, 128)) >> 3) & 7
    for f in range(4):
        for t in range(4):
            last = adj_ref[f, 0, 3, :, tile(t)]
            last = pltpu.roll(last, 72, 1)
            first = adj_ref[f, 0, 0, :, tile(t)]
            for a in range(1, 8):
                other = adj_ref[f, a, 3, :, tile(t)]
                last = jnp.where(j == a, pltpu.roll(other, (72 + 8 * a) % 128, 1), last)
                other = adj_ref[f, a, 0, :, tile(t)]
                first = jnp.where(j == a, pltpu.roll(other, 8 * a, 1), first)
            last_cross[f, :, tile(t)] = last
            first_cross[f, :, tile(t)] = first


def volume_kernel(
    node_ref, residual_ref, adj_ref, gx_ref, gyz_ref, out_ref, state, high, low, slope_x, slope_y, slope_z, ground
):
    order = (2, 0, 3, 1)
    row = {f: 128 * n for n, f in enumerate(order)}
    state[:, 0] = jnp.zeros((4, 16, 512), F32)
    state[:, 9] = jnp.zeros((4, 16, 512), F32)

    def load(a, carry):
        for f in range(4):
            for c in range(4):
                state[f, a + 1, 4 * c : 4 * c + 4, :] = adj_ref[f, a, c]
            rows = pl.ds(pl.multiple_of(row[f] + a * 16, 16), 16)
            high[rows], low[rows] = split(state[f, a + 1])
        return carry

    lax.fori_loop(0, 8, load, 0)
    for c in range(2):
        part = slice(256 * c, 256 * c + 256)
        slope_x[:, part] = product(high[...], low[...], gx_ref[0, :, part], gx_ref[1, :, part])
        slope_y[:, part] = product(
            high[0:256, part], low[0:256, part], gyz_ref[0, 0:256], gyz_ref[1, 0:256]
        )
        slope_z[:, part] = product(
            high[128:384, part], low[128:384, part], gyz_ref[0, 256:512], gyz_ref[1, 256:512]
        )

    node = node_ref[...]
    residual = residual_ref[...]
    target = lax.broadcasted_iota(jnp.int32, (128, 128), 0)
    spread = jnp.where(target == 4 * (node >> 6), residual, 0.0)
    place = lax.broadcasted_iota(jnp.int32, (512, 128), 0) == 8 * (node & 63)
    place = jnp.where(place, 1.0, 0.0).astype(BF16)
    ones, rest = split(spread)
    twos = (spread - ones.astype(F32) - rest.astype(F32)).astype(BF16)

    def match(a):
        return lax.dot_general(a, place, (((1,), (1,)), ((), ())), preferred_element_type=F32)

    ground[...] = match(ones) + (match(rest) + match(twos))

    lane = lanes((8, 128))
    sub = lax.broadcasted_iota(jnp.int32, (8, 128), 0)
    j = (lane >> 3) & 7
    k = lane & 7
    e = sub & 3
    odd = sub >= 4
    top_y = j == 7
    top_z = k == 7
    floor = e == 0
    ceiling = e == 3
    zero = jnp.zeros((8, 128), F32)
    sign_y = jnp.where(j == 0, HALF_LIFT, jnp.where(top_y, -HALF_LIFT, 0.0))
    size_y = jnp.where((j == 0) | top_y, -HALF_LIFT * ALPHA, 0.0)
    sign_z = jnp.where(k == 0, HALF_LIFT, jnp.where(top_z, -HALF_LIFT, 0.0))
    size_z = jnp.where((k == 0) | top_z, -HALF_LIFT * ALPHA, 0.0)

    def step(a, carry):
        for t in range(4):
            here = tile(t)
            q = [[state[f, a + 1, 8 * g : 8 * g + 8, here] for g in range(2)] for f in range(4)]
            dy = [[None] * 2 for _ in range(4)]
            dz = [[None] * 2 for _ in range(4)]
            dx = [[None] * 2 for _ in range(4)]
            for f in range(4):
                swap = [pltpu.roll(q[f][g], 4, 0) for g in range(2)]
                before = [jnp.where(odd, swap[0], zero), jnp.where(odd, swap[1], swap[0])]
                after = [jnp.where(odd, swap[1], swap[0]), jnp.where(odd, zero, swap[1])]
                for g in range(2):
                    x = q[f][g]
                    outer = jnp.where(top_y, pltpu.roll(after[g], 56, 1), pltpu.roll(before[g], 72, 1))
                    dy[f][g] = x - outer
                    below = pltpu.roll(pltpu.roll(x, 1, 0), 121, 1)
                    below = jnp.where(floor, -x if f == 3 else x, below)
                    above = pltpu.roll(pltpu.roll(x, 7, 0), 7, 1)
                    above = jnp.where(ceiling, zero, above)
                    dz[f][g] = x - jnp.where(top_z, above, below)
                    if t == 0:
                        outer = pltpu.roll(state[f, a, 8 * g : 8 * g + 8, tile(3)], 64, 1)
                        dx[f][g] = jnp.where(lane < 64, x - outer, zero)
                    if t == 3:
                        outer = pltpu.roll(state[f, a + 2, 8 * g : 8 * g + 8, tile(0)], 64, 1)
                        dx[f][g] = jnp.where(lane >= 64, x - outer, zero)
            for g in range(2):
                def rows(f, base=0):
                    return pl.ds(pl.multiple_of(row[f] - base + a * 16 + 8 * g, 8), 8)

                gx = [slope_x[rows(f), here] for f in range(4)]
                gy = {f: slope_y[rows(f), here] for f in (2, 0)}
                gz = {f: slope_z[rows(f, 128), here] for f in (0, 3)}
                rate = [
                    MACH * gx[0] + gx[1] + gy[2] + gz[3],
                    MACH * gx[1] + gx[0],
                    MACH * gx[2] + gy[0],
                    MACH * gx[3] + gz[0],
                ]
                for f in range(4):
                    rate[f] = rate[f] + size_y * dy[f][g] + size_z * dz[f][g]
                rate[0] = rate[0] + sign_y * dy[2][g] + sign_z * dz[3][g]
                rate[2] = rate[2] + sign_y * dy[0][g]
                rate[3] = rate[3] + sign_z * dz[0][g]
                if t in (0, 3):
                    s = -1.0 if t == 0 else 1.0
                    d = [dx[f][g] for f in range(4)]
                    own = -HALF_LIFT * (s * MACH + ALPHA)
                    rate[0] = rate[0] + own * d[0] - (HALF_LIFT * s) * d[1]
                    rate[1] = rate[1] + own * d[1] - (HALF_LIFT * s) * d[0]
                    rate[2] = rate[2] + own * d[2]
                    rate[3] = rate[3] + own * d[3]
                new = [q[f][g] + TIME_STEP * rate[f] for f in range(4)]
                source = ground[pl.ds(pl.multiple_of(a * 16 + 8 * g, 8), 8), here]
                new[0] = new[0] + (TIME_STEP * SOURCE_GAIN) * source
                for f in range(4):
                    out_ref[f, a, 8 * g : 8 * g + 8, here] = new[f]
        return carry

    lax.fori_loop(0, 8, step, 0)


def finish_kernel(
    arrival_ref, adj_ref, new_ref, before_along, after_along, before_cross, after_cross, received_ref,
    next_ref, kappa_ref, edge,
):
    lift = TIME_STEP * HALF_LIFT
    lane = lanes((4, 128))
    j = (lane >> 3) & 7

    def along_terms(ref, s, rows):
        q = [pltpu.roll(ref[f, rows, :], 64, 1) for f in range(4)]
        own = lift * (s * MACH + ALPHA)
        return [own * q[0] + (lift * s) * q[1], own * q[1] + (lift * s) * q[0], own * q[2], own * q[3]]

    def cross_terms(ref, s, t):
        q = [ref[f, :, tile(t)] for f in range(4)]
        own = lift * ALPHA
        return [
            own * q[0] + (lift * s) * q[2], own * q[1], own * q[2] + (lift * s) * q[0], own * q[3],
        ]

    for c in range(4):
        rows = slice(4 * c, 4 * c + 4)
        low = along_terms(before_along, -1.0, rows)
        high = along_terms(after_along, 1.0, rows)
        for f in range(4):
            edge[0, f, rows, :] = jnp.where(lane < 64, low[f], 0.0)
            edge[1, f, rows, :] = jnp.where(lane >= 64, high[f], 0.0)
    for t in range(4):
        low = cross_terms(before_cross, -1.0, t)
        high = cross_terms(after_cross, 1.0, t)
        for a in range(8):
            for f in range(4):
                for c in range(4):
                    value = new_ref[f, a, 4 * c : 4 * c + 4, tile(t)]
                    if c == 0:
                        value = value + jnp.where(j == 0, pltpu.roll(low[f], (128 - 8 * a) % 128, 1), 0.0)
                    if c == 3:
                        value = value + jnp.where(j == 7, pltpu.roll(high[f], (56 - 8 * a) % 128, 1), 0.0)
                    if t == 0 and a == 0:
                        value = value + edge[0, f, 4 * c : 4 * c + 4, :]
                    if t == 3 and a == 7:
                        value = value + edge[1, f, 4 * c : 4 * c + 4, :]
                    next_ref[f, a, c, :, tile(t)] = value
    for a in range(8):
        for c in range(4):
            q = arrival_ref[a, c]
            clipped = jnp.maximum(q, 0)
            holder = clipped >> 1
            second = (clipped & 1) == 1
            block = jnp.where(second, received_ref[holder, 4:8, :], received_ref[holder, 0:4, :])
            value = TIME_STEP * adj_ref[0, a, c] * block
            kappa_ref[a, c] = jnp.where(q >= 0, value, 0.0)


VMEM = pl.BlockSpec(memory_space=pltpu.VMEM)
SMEM = pl.BlockSpec(memory_space=pltpu.SMEM)


def kernel(body, out_shape, in_specs, scratch, flops, moved):
    return pl.pallas_call(
        body,
        out_shape=out_shape,
        in_specs=in_specs,
        out_specs=jax.tree.map(lambda _: VMEM, out_shape),
        scratch_shapes=scratch,
        compiler_params=pltpu.CompilerParams(vmem_limit_bytes=VMEM_BYTES),
        cost_estimate=pl.CostEstimate(flops=flops, bytes_accessed=moved, transcendentals=0),
    )


def array(*shape):
    return jax.ShapeDtypeStruct(shape, F32)


def shift(value, axis, up):
    peers = lax.axis_size(axis)
    pairs = [(i, i + 1) for i in range(peers - 1)]
    if not up:
        pairs = [(j, i) for i, j in pairs]
    return lax.ppermute(value, axis, pairs)


def per_device(adjoint_state, snapshot_store, dispatch_slot, arrival_slot, mic_node, mic_residual):
    gx, gyz = (jnp.asarray(table) for table in derivative_tables())
    outgoing, last_along, first_along, last_cross, first_cross = kernel(
        holder_kernel,
        (array(32, 8, 512), array(4, 16, 128), array(4, 16, 128), array(4, 4, 512), array(4, 4, 512)),
        [SMEM, VMEM, VMEM, VMEM, VMEM],
        [
            pltpu.VMEM((3, 16, 16, 512), F32),
            pltpu.VMEM((3, 256, 512), BF16),
            pltpu.VMEM((3, 256, 512), BF16),
        ],
        3_000_000_000, 5_000_000,
    )(dispatch_slot, adjoint_state, snapshot_store, gx, gyz)
    received = lax.all_to_all(outgoing, "cross", split_axis=0, concat_axis=0, tiled=True)
    before_along = shift(last_along, "along", True)
    after_along = shift(first_along, "along", False)
    before_cross = shift(last_cross, "cross", True)
    after_cross = shift(first_cross, "cross", False)
    updated = kernel(
        volume_kernel,
        array(4, 8, 16, 512),
        [VMEM] * 5,
        [
            pltpu.VMEM((4, 10, 16, 512), F32),
            pltpu.VMEM((512, 512), BF16),
            pltpu.VMEM((512, 512), BF16),
            pltpu.VMEM((512, 512), F32),
            pltpu.VMEM((256, 512), F32),
            pltpu.VMEM((256, 512), F32),
            pltpu.VMEM((128, 512), F32),
        ],
        4_000_000_000, 4_000_000,
    )(mic_node.reshape(1, 128), mic_residual.reshape(1, 128), adjoint_state, gx, gyz)
    return kernel(
        finish_kernel,
        (array(4, 8, 4, 4, 512), array(8, 4, 4, 512)),
        [SMEM] + [VMEM] * 7,
        [pltpu.VMEM((2, 4, 16, 128), F32)],
        10_000_000, 4_000_000,
    )(
        arrival_slot, adjoint_state, updated, before_along, after_along, before_cross, after_cross, received
    )


def solution(mesh):
    in_specs = (
        P(None, "along", "cross", None, None),
        P(("along", "cross"), None, None, None),
        P(("along", "cross")),
        P("along", "cross"),
        P(("along", "cross")),
        P(("along", "cross")),
    )
    out_specs = (P(None, "along", "cross", None, None), P("along", "cross", None, None))
    return jax.shard_map(
        per_device, mesh=mesh, in_specs=in_specs, out_specs=out_specs, check_vma=False
    )
```

time: 1010 us -> 42.7 us (0.04)
  the two profiles are of different devices: /device:TPU:32 before, /device:TPU:6 now
where the time goes in v1:
time: 42.7 us; the launch traced here: 42.3 us
  starting transfers between devices  26.1 us (61%)
  Pallas kernels  8.54 us (20%)
  local copies, waits for them, and re-layouts  6.87 us (16%)
  between operations  0.77 us (2%)
    ppermute x4, starting transfers between devices, shift(): return lax.ppermute(value, axis, pairs)  15 us
    all_to_all x1, starting transfers between devices, per_device(): lax.all_to_all(outgoing, 'cross', split_axis=0, concat_axis=0, tiled=True)  11.1 us
    unnamed x23, local copies, waits for them, and re-layouts  6.87 us
    pallas_call x1, Pallas kernels, per_device(): kernel(volume_kernel, array(4, 8, 16, 512), [VMEM] * 5, [pltpu.VMEM((4, 1...  3.63 us
    pallas_call x1, Pallas kernels, per_device(): kernel(holder_kernel, (array(32, 8, 512), array(4, 16, 128), array(4, 16,...  2.86 us
    pallas_call x1, Pallas kernels, per_device(): kernel(finish_kernel, (array(4, 8, 4, 4, 512), array(8, 4, 4, 512)), [SME...  2.06 us
  transfers between devices with their start and end apart: 5, of which 0 were waited for; matrix products, arithmetic and copies ran while one was open for 0% of the time, Pallas kernels for 9%

profile of v1, /device:TPU:6, one launch (start us, length us, event | category | flops | bytes accessed | tf_op | source)
XLA Modules:
  0.0 42.3 jit_solution(12657673057615295028)
XLA Ops:
  0.6 0.0 copy-start
  0.6 1.2 %copy-done = f32[4,8,4,4,512]{4,3,2,1,0:T(4,128)S(1)} copy-done((f32[4,8,4,4,512]{4,3,2,1,0:T(4,128)S(1)}, f32[4,8,4,4,512]{4,3,2,1,0:T(4,128)}, u32[]{:S(2)}) %copy-start) | copy-done | bytes 1048600
  1.9 1.4 %copy-done.2 = f32[64,3,4,512]{3,2,1,0:T(4,128)S(1)} copy-done((f32[64,3,4,512]{3,2,1,0:T(4,128)S(1)}, f32[64,3,4,512]{3,2,1,0:T(4,128)}, u32[]{:S(2)}) %copy-start.2) | copy-done | bytes 1572888
  3.3 0.7 %copy-done.3 = s32[64]{0:T(128)S(1)} copy-done((s32[64]{0:T(128)S(1)}, s32[64]{0:T(128)}, u32[]{:S(2)}) %copy-start.3) | copy-done | bytes 280
  3.9 1.2 %copy-done.6 = bf16[2,512,512]{2,1,0:T(8,128)(2,1)S(1)} copy-done((bf16[2,512,512]{2,1,0:T(8,128)(2,1)S(1)}, bf16[2,512,512]{2,1,0:T(8,128)(2,1)}, u32[]{:S(2)}) %copy-start.6) | copy-done | bytes 1048600
  5.1 1.0 %copy-done.8 = bf16[2,512,256]{2,1,0:T(8,128)(2,1)S(1)} copy-done((bf16[2,512,256]{2,1,0:T(8,128)(2,1)S(1)}, bf16[2,512,256]{2,1,0:T(8,128)(2,1)}, u32[]{:S(2)}) %copy-start.8) | copy-done | bytes 524312
  6.2 2.9 %shard_map.96 = (f32[32,8,512]{2,1,0:T(8,128)}, f32[4,16,128]{2,1,0:T(8,128)S(1)}, f32[4,16,128]{2,1,0:T(8,128)S(1)}, f32[4,4,512]{2,1,0:T(4,128)S(1)}, f32[4,4,512]{2,1,0:T(4,128)S(1)}) custom-call(s32[64]{0:T(128)S(1)} %copy-done.3, f32[4,8,4,4,512]{4,3,2,1,0:T(4,128)S(1)} %copy-done, f32[64,3,4,512]{3,2,1,0:T(4,128)S(1)} %copy-done.2, ...), custom_call_target="tpu_custom_call" | custom-call | flops 3000000000 | bytes 5000000 | tf_op jit(solution)/shard_map/pallas_call | solution.py:326
  9.1 11.1 %all-to-all-start = ((f32[32,8,512]{2,1,0:T(8,128)}), f32[32,8,512]{2,1,0:T(8,128)S(1)}, u32[]{:S(2)}, u32[]{:S(2)}) async-start(f32[32,8,512]{2,1,0:T(8,128)} %get-tuple-element.11), calls=%async_computation | async-start | bytes 1048576 | tf_op jit(solution)/shard_map/all_to_all | solution.py:337
  20.1 1.9 %collective-permute-start = (f32[4,16,128]{2,1,0:T(8,128)S(1)}, f32[4,16,128]{2,1,0:T(8,128)S(1)}, u32[]{:S(2)}, u32[]{:S(2)}) collective-permute-start(f32[4,16,128]{2,1,0:T(8,128)S(1)} %get-tuple-element.7), channel_id=1, source_target_pairs={{0,32},{32,64},{64,96},{1,33},{33,65},{65,97},{2,34},{34,66},{66,9... | collective-permute-start | bytes 98312 | tf_op jit(solution)/shard_map/ppermute | solution.py:321
  22.1 3.6 %collective-permute-start.1 = (f32[4,16,128]{2,1,0:T(8,128)S(1)}, f32[4,16,128]{2,1,0:T(8,128)S(1)}, u32[]{:S(2)}, u32[]{:S(2)}) collective-permute-start(f32[4,16,128]{2,1,0:T(8,128)S(1)} %get-tuple-element.8), channel_id=1, source_target_pairs={{32,0},{64,32},{96,64},{33,1},{65,33},{97,65},{34,2},{66,34},{98,6... | collective-permute-start | bytes 98312 | tf_op jit(solution)/shard_map/ppermute | solution.py:321
  25.7 3.4 %collective-permute-start.2 = (f32[4,4,512]{2,1,0:T(4,128)S(1)}, f32[4,4,512]{2,1,0:T(4,128)S(1)}, u32[]{:S(2)}, u32[]{:S(2)}) collective-permute-start(f32[4,4,512]{2,1,0:T(4,128)S(1)} %get-tuple-element.9), channel_id=1, source_target_pairs={{0,1},{1,2},{2,3},{3,4},{4,5},{5,6},{6,7},{7,8},{8,9},{9,10},{10,1... | collective-permute-start | bytes 98312 | tf_op jit(solution)/shard_map/ppermute | solution.py:321
  29.1 6.1 %collective-permute-start.3 = (f32[4,4,512]{2,1,0:T(4,128)S(1)}, f32[4,4,512]{2,1,0:T(4,128)S(1)}, u32[]{:S(2)}, u32[]{:S(2)}) collective-permute-start(f32[4,4,512]{2,1,0:T(4,128)S(1)} %get-tuple-element.10), channel_id=1, source_target_pairs={{1,0},{2,1},{3,2},{4,3},{5,4},{6,5},{7,6},{8,7},{9,8},{10,9},{11,1... | collective-permute-start | bytes 98312 | tf_op jit(solution)/shard_map/ppermute | solution.py:321
  35.2 0.0 copy-done.1
  35.2 0.0 copy-start.7
  35.2 1.2 %copy-done.7 = bf16[2,512,512]{2,1,0:T(8,128)(2,1)S(1)} copy-done((bf16[2,512,512]{2,1,0:T(8,128)(2,1)S(1)}, bf16[2,512,512]{2,1,0:T(8,128)(2,1)}, u32[]{:S(2)}) %copy-start.7) | copy-done | bytes 1048600
  36.5 3.6 %shard_map.95.new_ref = f32[4,8,16,512]{3,2,1,0:T(8,128)S(1)} custom-call(s32[1,128]{1,0:T(1,128)S(1)} %bitcast.2, f32[1,128]{1,0:T(1,128)S(1)} %bitcast.3, f32[4,8,4,4,512]{4,3,2,1,0:T(4,128)S(1)} %copy-done.1, bf16[2,512,512]{2,1,0:T(8,128)(2,1)S(1)} %copy-done.7, bf16[2,512,256]{2,1,0:T(8,128)(2,1)S(1)} %copy-done.9), custom_call_target="tpu_custom_call" | custom-call | flops 4000000000 | bytes 4000000 | tf_op jit(solution)/shard_map/pallas_call | solution.py:342
  40.1 0.0 copy-done.10
  40.1 0.1 copy.10.arrival_ref
  40.2 0.0 collective-permute-done.before_along
  40.2 0.0 collective-permute-done.1.after_along
  40.2 0.0 collective-permute-done.2.before_cross
  40.2 0.0 collective-permute-done.3.after_cross
  40.2 0.0 all-to-all-done.received_ref
  40.2 2.1 %shard_map.97 = (f32[4,8,4,4,512]{4,3,2,1,0:T(4,128)}, f32[8,4,4,512]{3,2,1,0:T(4,128)}) custom-call(s32[8,4]{1,0:T(8,128)S(1)} %copy.10.arrival_ref, f32[4,8,4,4,512]{4,3,2,1,0:T(4,128)S(1)} %copy-done.1, f32[4,8,16,512]{3,2,1,0:T(8,128)S(1)} %shard_map.95.new_ref, f32[4,16,128]{2,1,0:T(8,128)S(1)} %collective-permute-done.before_along, ...), custom_call_target="tpu_custom_call" | custom-call | flops 10000000 | bytes 4000000 | tf_op jit(solution)/shard_map/pallas_call | solution.py:357
  (12 shorter events, 0.0 us)
Async XLA Ops:
  0.6 1.2 %copy-start = (f32[4,8,4,4,512]{4,3,2,1,0:T(4,128)S(1)}, f32[4,8,4,4,512]{4,3,2,1,0:T(4,128)}, u32[]{:S(2)}) copy-start(f32[4,8,4,4,512]{4,3,2,1,0:T(4,128)} %adj_ref.5) | copy-start | bytes 3145732
  1.9 1.4 %copy-start.2 = (f32[64,3,4,512]{3,2,1,0:T(4,128)S(1)}, f32[64,3,4,512]{3,2,1,0:T(4,128)}, u32[]{:S(2)}) copy-start(f32[64,3,4,512]{3,2,1,0:T(4,128)} %store_ref.1) | copy-start | bytes 4718596
  3.3 0.7 %copy-start.3 = (s32[64]{0:T(128)S(1)}, s32[64]{0:T(128)}, u32[]{:S(2)}) copy-start(s32[64]{0:T(128)} %slot_ref.1) | copy-start | bytes 772
  3.9 1.2 %copy-start.6 = (bf16[2,512,512]{2,1,0:T(8,128)(2,1)S(1)}, bf16[2,512,512]{2,1,0:T(8,128)(2,1)}, u32[]{:S(2)}) copy-start(bf16[2,512,512]{2,1,0:T(8,128)(2,1)} %constant.4.clone.gx_ref) | copy-start | bytes 3145732
  5.1 1.0 %copy-start.8 = (bf16[2,512,256]{2,1,0:T(8,128)(2,1)S(1)}, bf16[2,512,256]{2,1,0:T(8,128)(2,1)}, u32[]{:S(2)}) copy-start(bf16[2,512,256]{2,1,0:T(8,128)(2,1)} %constant.5.clone.gyz_ref) | copy-start | bytes 1572868
  6.2 29.0 %copy-start.1 = (f32[4,8,4,4,512]{4,3,2,1,0:T(4,128)S(1)}, f32[4,8,4,4,512]{4,3,2,1,0:T(4,128)}, u32[]{:S(2)}) copy-start(f32[4,8,4,4,512]{4,3,2,1,0:T(4,128)} %adj_ref.5) | copy-start | bytes 3145732
  6.2 29.0 %copy-start.4 = (s32[128]{0:T(128)S(1)}, s32[128]{0:T(128)}, u32[]{:S(2)}) copy-start(s32[128]{0:T(128)} %param.12) | copy-start | bytes 1540
  6.2 29.0 %copy-start.5 = (f32[128]{0:T(128)S(1)}, f32[128]{0:T(128)}, u32[]{:S(2)}) copy-start(f32[128]{0:T(128)} %param.13) | copy-start | bytes 1540
  6.2 29.0 %copy-start.9 = (bf16[2,512,256]{2,1,0:T(8,128)(2,1)S(1)}, bf16[2,512,256]{2,1,0:T(8,128)(2,1)}, u32[]{:S(2)}) copy-start(bf16[2,512,256]{2,1,0:T(8,128)(2,1)} %constant.5.clone.gyz_ref) | copy-start | bytes 1572868
  9.1 31.1 %all-to-all-start = ((f32[32,8,512]{2,1,0:T(8,128)}), f32[32,8,512]{2,1,0:T(8,128)S(1)}, u32[]{:S(2)}, u32[]{:S(2)}) async-start(f32[32,8,512]{2,1,0:T(8,128)} %get-tuple-element.11), calls=%async_computation | async-start | bytes 1048576 | tf_op jit(solution)/shard_map/all_to_all | solution.py:337
  20.1 20.1 %collective-permute-start = (f32[4,16,128]{2,1,0:T(8,128)S(1)}, f32[4,16,128]{2,1,0:T(8,128)S(1)}, u32[]{:S(2)}, u32[]{:S(2)}) collective-permute-start(f32[4,16,128]{2,1,0:T(8,128)S(1)} %get-tuple-element.7), channel_id=1, source_target_pairs={{0,32},{32,64},{64,96},{1,33},{33,65},{65,97},{2,34},{34,66},{66,9... | collective-permute-start | bytes 98312 | tf_op jit(solution)/shard_map/ppermute | solution.py:321
  22.1 18.1 %collective-permute-start.1 = (f32[4,16,128]{2,1,0:T(8,128)S(1)}, f32[4,16,128]{2,1,0:T(8,128)S(1)}, u32[]{:S(2)}, u32[]{:S(2)}) collective-permute-start(f32[4,16,128]{2,1,0:T(8,128)S(1)} %get-tuple-element.8), channel_id=1, source_target_pairs={{32,0},{64,32},{96,64},{33,1},{65,33},{97,65},{34,2},{66,34},{98,6... | collective-permute-start | bytes 98312 | tf_op jit(solution)/shard_map/ppermute | solution.py:321
  25.7 14.5 %collective-permute-start.2 = (f32[4,4,512]{2,1,0:T(4,128)S(1)}, f32[4,4,512]{2,1,0:T(4,128)S(1)}, u32[]{:S(2)}, u32[]{:S(2)}) collective-permute-start(f32[4,4,512]{2,1,0:T(4,128)S(1)} %get-tuple-element.9), channel_id=1, source_target_pairs={{0,1},{1,2},{2,3},{3,4},{4,5},{5,6},{6,7},{7,8},{8,9},{9,10},{10,1... | collective-permute-start | bytes 98312 | tf_op jit(solution)/shard_map/ppermute | solution.py:321
  29.1 11.1 %collective-permute-start.3 = (f32[4,4,512]{2,1,0:T(4,128)S(1)}, f32[4,4,512]{2,1,0:T(4,128)S(1)}, u32[]{:S(2)}, u32[]{:S(2)}) collective-permute-start(f32[4,4,512]{2,1,0:T(4,128)S(1)} %get-tuple-element.10), channel_id=1, source_target_pairs={{1,0},{2,1},{3,2},{4,3},{5,4},{6,5},{7,6},{8,7},{9,8},{10,9},{11,1... | collective-permute-start | bytes 98312 | tf_op jit(solution)/shard_map/ppermute | solution.py:321
  35.2 1.2 %copy-start.7 = (bf16[2,512,512]{2,1,0:T(8,128)(2,1)S(1)}, bf16[2,512,512]{2,1,0:T(8,128)(2,1)}, u32[]{:S(2)}) copy-start(bf16[2,512,512]{2,1,0:T(8,128)(2,1)} %constant.4.clone.gx_ref) | copy-start | bytes 3145732
  36.4 3.6 %copy-start.10 = (s32[8,4]{0,1:T(4,128)S(1)}, s32[8,4]{0,1:T(4,128)}, u32[]{:S(2)}) copy-start(s32[8,4]{0,1:T(4,128)} %param.11) | copy-start | bytes 388

commit v2 on v1

--- a/solution.py
+++ b/solution.py
@@ -23,6 +23,7 @@
 F32 = jnp.float32
 BF16 = jnp.bfloat16
 VMEM_BYTES = 24 * 1024 * 1024
+HOLDER_BYTES = 60_000_000
 
 
 def legendre_seven(points):
@@ -36,14 +37,7 @@
     return current
 
 
-def high_low(table):
-    table = table.astype(np.float32)
-    high = table.astype(BF16)
-    low = (table - high.astype(np.float32)).astype(BF16)
-    return np.stack([high, low])
-
-
-def derivative_tables():
+def derivative_rows():
     degree = 7
     points = np.array([-1.0] + LOBATTO_INNER + [1.0])
     values = legendre_seven(points)
@@ -52,10 +46,40 @@
     matrix = matrix * (1.0 - np.eye(degree + 1))
     matrix[0, 0] = -degree * (degree + 1) / 4.0
     matrix[degree, degree] = degree * (degree + 1) / 4.0
-    along = 2.0 * np.kron(matrix, np.eye(64))
-    cross = 2.0 * np.kron(np.kron(np.eye(4), matrix), np.eye(8))
-    vertical = 2.0 * np.kron(np.eye(32), matrix)
-    return high_low(along.T), high_low(np.concatenate([cross.T, vertical.T]))
+    twice = 2.0 * matrix.T
+    rows = np.stack(
+        [np.repeat(twice, 64, axis=1), np.tile(np.repeat(twice, 8, axis=1), 8), np.tile(twice, 64)]
+    ).astype(np.float32)
+    high = rows.astype(BF16)
+    low = (rows - high.astype(np.float32)).astype(BF16)
+    return np.stack([high, low]).astype(np.float32)
+
+
+def fill_table(rows_ref, table):
+    lane = lanes((16, 128))
+    sub = lax.broadcasted_iota(jnp.int32, (16, 128), 0)
+    upper = sub >= 8
+    zero = jnp.zeros((16, 128), F32)
+    for h in range(2):
+        for i in range(8):
+            for t in range(4):
+                row = rows_ref[h, 0, i : i + 1, tile(t)]
+                for m in range(4):
+                    value = jnp.where((lane & 63) == sub + 16 * m, row, zero)
+                    table[h, 64 * i + 16 * m : 64 * i + 16 * m + 16, tile(t)] = value.astype(BF16)
+        row = rows_ref[h, 2, :, tile(0)]
+        vertical = jnp.concatenate([row, row], axis=0)
+        for g in range(16):
+            here = g // 8
+            j = 2 * g % 8
+            row = jnp.where(upper, rows_ref[h, 1, j + 1 : j + 2, tile(0)], rows_ref[h, 1, j : j + 1, tile(0)])
+            inside = ((lane >> 6) == g // 4 % 2) & ((lane & 7) == (sub & 7))
+            cross = jnp.where(inside, row, zero).astype(BF16)
+            inside = (lane >> 3) == (sub >> 3) + 2 * (g % 8)
+            level = jnp.where(inside, vertical, zero).astype(BF16)
+            for t in range(2):
+                table[h, 16 * g : 16 * g + 16, tile(4 + t)] = cross if t == here else zero.astype(BF16)
+                table[h, 256 + 16 * g : 272 + 16 * g, tile(4 + t)] = level if t == here else zero.astype(BF16)
 
 
 def split(x):
@@ -78,11 +102,55 @@
     return slice(128 * t, 128 * t + 128)
 
 
+def is_even(axis):
+    return (lax.axis_index(axis) & 1) == 0
+
+
 def holder_kernel(
-    slot_ref, adj_ref, store_ref, gx_ref, gyz_ref,
-    out_ref, last_along, first_along, last_cross, first_cross,
-    stage, high, low,
+    slot_hbm, adj_hbm, store_hbm, rows_hbm,
+    out_hbm, along_one, along_two, cross_one, cross_two,
+    slot_ref, store_ref, rows_ref, table, face_along, face_cross, stage, high, low, total, sems,
 ):
+    pieces = [
+        (slot_hbm, slot_ref),
+        (store_hbm, store_ref),
+        (adj_hbm.at[:, 0, :, :, tile(0)], face_along.at[0]),
+        (adj_hbm.at[:, 7, :, :, tile(3)], face_along.at[1]),
+        (adj_hbm.at[:, :, 0], face_cross.at[0]),
+        (adj_hbm.at[:, :, 3], face_cross.at[1]),
+        (rows_hbm, rows_ref),
+    ]
+    copies = [pltpu.make_async_copy(src, dst, sems.at[n]) for n, (src, dst) in enumerate(pieces)]
+    for copy in copies:
+        copy.start()
+    for n in (2, 3, 4, 5):
+        copies[n].wait()
+    even = is_even("along")
+    for f in range(4):
+        for c in range(4):
+            rows = slice(4 * c, 4 * c + 4)
+            first = face_along[0, f, c]
+            last = face_along[1, f, c]
+            along_one[f, rows, :] = jnp.where(even, last, first)
+            along_two[f, rows, :] = jnp.where(even, first, last)
+    even = is_even("cross")
+    j = (lanes((4, 128)) >> 3) & 7
+    for f in range(4):
+        for t in range(4):
+            last = pltpu.roll(face_cross[1, f, 0, :, tile(t)], 72, 1)
+            first = face_cross[0, f, 0, :, tile(t)]
+            for a in range(1, 8):
+                other = face_cross[1, f, a, :, tile(t)]
+                last = jnp.where(j == a, pltpu.roll(other, (72 + 8 * a) % 128, 1), last)
+                other = face_cross[0, f, a, :, tile(t)]
+                first = jnp.where(j == a, pltpu.roll(other, 8 * a, 1), first)
+            cross_one[f, :, tile(t)] = jnp.where(even, last, first)
+            cross_two[f, :, tile(t)] = jnp.where(even, first, last)
+    copies[6].wait()
+    fill_table(rows_ref, table)
+    copies[0].wait()
+    copies[1].wait()
+
     def gather(g, carry):
         rows = pl.ds(pl.multiple_of(g * 16, 16), 16)
         for m in range(4):
@@ -94,35 +162,26 @@
         return carry
 
     lax.fori_loop(0, 16, gather, 0)
+    writes = []
     for c in range(2):
         part = slice(256 * c, 256 * c + 256)
-        total = product(high[0], low[0], gx_ref[0, :, part], gx_ref[1, :, part])
+        spread = product(high[0], low[0], table[0, :, part], table[1, :, part])
         for f in (1, 2):
             rows = slice(256 * (f - 1), 256 * f)
-            total += product(high[f, :, part], low[f, :, part], gyz_ref[0, rows], gyz_ref[1, rows])
-        out_ref[:, :, part] = total.reshape(32, 8, 256)
-    for f in range(4):
-        for c in range(4):
-            last_along[f, 4 * c : 4 * c + 4, :] = adj_ref[f, 7, c, :, tile(3)]
-            first_along[f, 4 * c : 4 * c + 4, :] = adj_ref[f, 0, c, :, tile(0)]
-    j = (lanes((4, 128)) >> 3) & 7
-    for f in range(4):
-        for t in range(4):
-            last = adj_ref[f, 0, 3, :, tile(t)]
-            last = pltpu.roll(last, 72, 1)
-            first = adj_ref[f, 0, 0, :, tile(t)]
-            for a in range(1, 8):
-                other = adj_ref[f, a, 3, :, tile(t)]
-                last = jnp.where(j == a, pltpu.roll(other, (72 + 8 * a) % 128, 1), last)
-                other = adj_ref[f, a, 0, :, tile(t)]
-                first = jnp.where(j == a, pltpu.roll(other, 8 * a, 1), first)
-            last_cross[f, :, tile(t)] = last
-            first_cross[f, :, tile(t)] = first
+            spread += product(high[f, :, part], low[f, :, part], table[0, rows, 512:768], table[1, rows, 512:768])
+        total[:, :, part] = spread.reshape(32, 8, 256)
+        writes.append(
+            pltpu.make_async_copy(total.at[:, :, part], out_hbm.at[:, :, part], sems.at[7 + c])
+        )
+        writes[c].start()
+    for write in writes:
+        write.wait()
 
 
 def volume_kernel(
-    node_ref, residual_ref, adj_ref, gx_ref, gyz_ref, out_ref, state, high, low, slope_x, slope_y, slope_z, ground
+    node_ref, residual_ref, adj_ref, rows_ref, out_ref, table, state, high, low, slope_x, slope_y, slope_z, ground
 ):
+    fill_table(rows_ref, table)
     order = (2, 0, 3, 1)
     row = {f: 128 * n for n, f in enumerate(order)}
     state[:, 0] = jnp.zeros((4, 16, 512), F32)
@@ -139,12 +198,12 @@
     lax.fori_loop(0, 8, load, 0)
     for c in range(2):
         part = slice(256 * c, 256 * c + 256)
-        slope_x[:, part] = product(high[...], low[...], gx_ref[0, :, part], gx_ref[1, :, part])
+        slope_x[:, part] = product(high[...], low[...], table[0, :, part], table[1, :, part])
         slope_y[:, part] = product(
-            high[0:256, part], low[0:256, part], gyz_ref[0, 0:256], gyz_ref[1, 0:256]
+            high[0:256, part], low[0:256, part], table[0, 0:256, 512:768], table[1, 0:256, 512:768]
         )
         slope_z[:, part] = product(
-            high[128:384, part], low[128:384, part], gyz_ref[0, 256:512], gyz_ref[1, 256:512]
+            high[128:384, part], low[128:384, part], table[0, 256:512, 512:768], table[1, 256:512, 512:768]
         )
 
     node = node_ref[...]
@@ -240,20 +299,25 @@
 
 
 def finish_kernel(
-    arrival_ref, adj_ref, new_ref, before_along, after_along, before_cross, after_cross, received_ref,
+    arrival_ref, adj_ref, new_ref, along_one, along_two, cross_one, cross_two, received_ref,
     next_ref, kappa_ref, edge,
 ):
     lift = TIME_STEP * HALF_LIFT
     lane = lanes((4, 128))
     j = (lane >> 3) & 7
 
-    def along_terms(ref, s, rows):
-        q = [pltpu.roll(ref[f, rows, :], 64, 1) for f in range(4)]
+    def arrived(axis, one, two, s, f, index):
+        use_one = is_even(axis) if s > 0 else jnp.logical_not(is_even(axis))
+        return jnp.where(use_one, one[(f, *index)], two[(f, *index)])
+
+    def along_terms(s, rows):
+        q = [arrived("along", along_one, along_two, s, f, (rows, slice(None))) for f in range(4)]
+        q = [pltpu.roll(x, 64, 1) for x in q]
         own = lift * (s * MACH + ALPHA)
         return [own * q[0] + (lift * s) * q[1], own * q[1] + (lift * s) * q[0], own * q[2], own * q[3]]
 
-    def cross_terms(ref, s, t):
-        q = [ref[f, :, tile(t)] for f in range(4)]
+    def cross_terms(s, t):
+        q = [arrived("cross", cross_one, cross_two, s, f, (slice(None), tile(t))) for f in range(4)]
         own = lift * ALPHA
         return [
             own * q[0] + (lift * s) * q[2], own * q[1], own * q[2] + (lift * s) * q[0], own * q[3],
@@ -261,14 +325,14 @@
 
     for c in range(4):
         rows = slice(4 * c, 4 * c + 4)
-        low = along_terms(before_along, -1.0, rows)
-        high = along_terms(after_along, 1.0, rows)
+        low = along_terms(-1.0, rows)
+        high = along_terms(1.0, rows)
         for f in range(4):
             edge[0, f, rows, :] = jnp.where(lane < 64, low[f], 0.0)
             edge[1, f, rows, :] = jnp.where(lane >= 64, high[f], 0.0)
     for t in range(4):
-        low = cross_terms(before_cross, -1.0, t)
-        high = cross_terms(after_cross, 1.0, t)
+        low = cross_terms(-1.0, t)
+        high = cross_terms(1.0, t)
         for a in range(8):
             for f in range(4):
                 for c in range(4):
@@ -294,17 +358,18 @@
 
 
 VMEM = pl.BlockSpec(memory_space=pltpu.VMEM)
+HBM = pl.BlockSpec(memory_space=pltpu.HBM)
 SMEM = pl.BlockSpec(memory_space=pltpu.SMEM)
 
 
-def kernel(body, out_shape, in_specs, scratch, flops, moved):
+def kernel(body, out_shape, in_specs, scratch, flops, moved, out_specs=None, limit=VMEM_BYTES):
     return pl.pallas_call(
         body,
         out_shape=out_shape,
         in_specs=in_specs,
-        out_specs=jax.tree.map(lambda _: VMEM, out_shape),
+        out_specs=out_specs or jax.tree.map(lambda _: VMEM, out_shape),
         scratch_shapes=scratch,
-        compiler_params=pltpu.CompilerParams(vmem_limit_bytes=VMEM_BYTES),
+        compiler_params=pltpu.CompilerParams(vmem_limit_bytes=limit),
         cost_estimate=pl.CostEstimate(flops=flops, bytes_accessed=moved, transcendentals=0),
     )
 
@@ -313,37 +378,47 @@
     return jax.ShapeDtypeStruct(shape, F32)
 
 
-def shift(value, axis, up):
-    peers = lax.axis_size(axis)
-    pairs = [(i, i + 1) for i in range(peers - 1)]
-    if not up:
-        pairs = [(j, i) for i, j in pairs]
+def exchange(value, axis, start):
+    pairs = []
+    for i in range(start, lax.axis_size(axis) - 1, 2):
+        pairs += [(i, i + 1), (i + 1, i)]
     return lax.ppermute(value, axis, pairs)
 
 
 def per_device(adjoint_state, snapshot_store, dispatch_slot, arrival_slot, mic_node, mic_residual):
-    gx, gyz = (jnp.asarray(table) for table in derivative_tables())
-    outgoing, last_along, first_along, last_cross, first_cross = kernel(
+    rows = jnp.asarray(derivative_rows())
+    outgoing, along_one, along_two, cross_one, cross_two = kernel(
         holder_kernel,
         (array(32, 8, 512), array(4, 16, 128), array(4, 16, 128), array(4, 4, 512), array(4, 4, 512)),
-        [SMEM, VMEM, VMEM, VMEM, VMEM],
+        [HBM] * 4,
         [
+            pltpu.SMEM((64,), jnp.int32),
+            pltpu.VMEM((64, 3, 4, 512), F32),
+            pltpu.VMEM((2, 3, 8, 512), F32),
+            pltpu.VMEM((2, 512, 768), BF16),
+            pltpu.VMEM((2, 4, 4, 4, 128), F32),
+            pltpu.VMEM((2, 4, 8, 4, 512), F32),
             pltpu.VMEM((3, 16, 16, 512), F32),
             pltpu.VMEM((3, 256, 512), BF16),
             pltpu.VMEM((3, 256, 512), BF16),
+            pltpu.VMEM((32, 8, 512), F32),
+            pltpu.SemaphoreType.DMA((9,)),
         ],
         3_000_000_000, 5_000_000,
-    )(dispatch_slot, adjoint_state, snapshot_store, gx, gyz)
+        (HBM, VMEM, VMEM, VMEM, VMEM),
+        HOLDER_BYTES,
+    )(dispatch_slot, adjoint_state, snapshot_store, rows)
     received = lax.all_to_all(outgoing, "cross", split_axis=0, concat_axis=0, tiled=True)
-    before_along = shift(last_along, "along", True)
-    after_along = shift(first_along, "along", False)
-    before_cross = shift(last_cross, "cross", True)
-    after_cross = shift(first_cross, "cross", False)
+    along_one = exchange(along_one, "along", 0)
+    along_two = exchange(along_two, "along", 1)
+    cross_one = exchange(cross_one, "cross", 0)
+    cross_two = exchange(cross_two, "cross", 1)
     updated = kernel(
         volume_kernel,
         array(4, 8, 16, 512),
-        [VMEM] * 5,
+        [VMEM] * 4,
         [
+            pltpu.VMEM((2, 512, 768), BF16),
             pltpu.VMEM((4, 10, 16, 512), F32),
             pltpu.VMEM((512, 512), BF16),
             pltpu.VMEM((512, 512), BF16),
@@ -353,7 +428,7 @@
             pltpu.VMEM((128, 512), F32),
         ],
         4_000_000_000, 4_000_000,
-    )(mic_node.reshape(1, 128), mic_residual.reshape(1, 128), adjoint_state, gx, gyz)
+    )(mic_node.reshape(1, 128), mic_residual.reshape(1, 128), adjoint_state, rows)
     return kernel(
         finish_kernel,
         (array(4, 8, 4, 4, 512), array(8, 4, 4, 512)),
@@ -361,7 +436,7 @@
         [pltpu.VMEM((2, 4, 16, 128), F32)],
         10_000_000, 4_000_000,
     )(
-        arrival_slot, adjoint_state, updated, before_along, after_along, before_cross, after_cross, received
+        arrival_slot, adjoint_state, updated, along_one, along_two, cross_one, cross_two, received
     )
 
 

time: 42.7 us -> 33.8 us (0.79)
  the two profiles are of different devices: /device:TPU:6 before, /device:TPU:33 now
where the time goes in v2:
time: 33.8 us; the launch traced here: 33.5 us
  starting transfers between devices  21.5 us (64%)
  Pallas kernels  11.1 us (33%)
  between operations  0.77 us (2%)
    ppermute x4, starting transfers between devices, exchange(): return lax.ppermute(value, axis, pairs)  11.4 us
    all_to_all x1, starting transfers between devices, per_device(): lax.all_to_all(outgoing, 'cross', split_axis=0, concat_axis=0, tiled=True)  10.1 us
    pallas_call x1, Pallas kernels, per_device(): kernel(holder_kernel, (array(32, 8, 512), array(4, 16, 128), array(4, 16,...  5.18 us
    pallas_call x1, Pallas kernels, per_device(): kernel(volume_kernel, array(4, 8, 16, 512), [VMEM] * 4, [pltpu.VMEM((2, 5...  3.85 us
    pallas_call x1, Pallas kernels, per_device(): kernel(finish_kernel, (array(4, 8, 4, 4, 512), array(8, 4, 4, 512)), [SME...  2.07 us
  transfers between devices with their start and end apart: 5, of which 0 were waited for; matrix products, arithmetic and copies ran while one was open for 0% of the time, Pallas kernels for 11%

profile of v2, /device:TPU:33, one launch (start us, length us, event | category | flops | bytes accessed | tf_op | source)
XLA Modules:
  0.0 33.5 jit_solution(15904720927682666380)
XLA Ops:
  0.6 0.0 copy-start.3
  0.6 0.0 copy-start
  0.7 0.0 copy-start.2
  0.7 0.0 copy-start.1
  0.7 5.2 %shard_map.87 = (f32[32,8,512]{2,1,0:T(8,128)}, f32[4,16,128]{2,1,0:T(8,128)}, f32[4,16,128]{2,1,0:T(8,128)}, f32[4,4,512]{2,1,0:T(4,128)}, f32[4,4,512]{2,1,0:T(4,128)}) custom-call(s32[64]{0:T(128)} %slot_hbm.1, f32[4,8,4,4,512]{4,3,2,1,0:T(4,128)} %adj_ref.3, f32[64,3,4,512]{3,2,1,0:T(4,128)} %store_hbm.1, f32[2,3,8,512]{3,2,1,0:T(8,128)} %constant.2.clone.rows_ref.rows_hbm), custom_call_target="tpu_custom_call" | custom-call | flops 3000000000 | bytes 5000000 | tf_op jit(solution)/shard_map/pallas_call | solution.py:390
  5.9 10.1 %all-to-all-start = ((f32[32,8,512]{2,1,0:T(8,128)}), f32[32,8,512]{2,1,0:T(8,128)S(1)}, u32[]{:S(2)}, u32[]{:S(2)}) async-start(f32[32,8,512]{2,1,0:T(8,128)} %get-tuple-element.11), calls=%async_computation | async-start | bytes 1048576 | tf_op jit(solution)/shard_map/all_to_all | solution.py:411
  16.0 1.3 %collective-permute-start = (f32[4,16,128]{2,1,0:T(8,128)}, f32[4,16,128]{2,1,0:T(8,128)S(1)}, u32[]{:S(2)}, u32[]{:S(2)}) collective-permute-start(f32[4,16,128]{2,1,0:T(8,128)} %get-tuple-element.7), channel_id=1, source_target_pairs={{0,32},{32,0},{64,96},{96,64},{1,33},{33,1},{65,97},{97,65},{2,34}... | collective-permute-start | bytes 98312 | tf_op jit(solution)/shard_map/ppermute | solution.py:385
  17.3 2.1 %collective-permute-start.1 = (f32[4,16,128]{2,1,0:T(8,128)}, f32[4,16,128]{2,1,0:T(8,128)S(1)}, u32[]{:S(2)}, u32[]{:S(2)}) collective-permute-start(f32[4,16,128]{2,1,0:T(8,128)} %get-tuple-element.8), channel_id=1, source_target_pairs={{32,64},{64,32},{33,65},{65,33},{34,66},{66,34},{35,67},{67,35},{3... | collective-permute-start | bytes 98312 | tf_op jit(solution)/shard_map/ppermute | solution.py:385
  19.4 1.3 %collective-permute-start.2 = (f32[4,4,512]{2,1,0:T(4,128)}, f32[4,4,512]{2,1,0:T(4,128)S(1)}, u32[]{:S(2)}, u32[]{:S(2)}) collective-permute-start(f32[4,4,512]{2,1,0:T(4,128)} %get-tuple-element.9), channel_id=1, source_target_pairs={{0,1},{1,0},{2,3},{3,2},{4,5},{5,4},{6,7},{7,6},{8,9},{9,8},{10,11... | collective-permute-start | bytes 98312 | tf_op jit(solution)/shard_map/ppermute | solution.py:385
  20.7 6.7 %collective-permute-start.3 = (f32[4,4,512]{2,1,0:T(4,128)}, f32[4,4,512]{2,1,0:T(4,128)S(1)}, u32[]{:S(2)}, u32[]{:S(2)}) collective-permute-start(f32[4,4,512]{2,1,0:T(4,128)} %get-tuple-element.10), channel_id=1, source_target_pairs={{1,2},{2,1},{3,4},{4,3},{5,6},{6,5},{7,8},{8,7},{9,10},{10,9},{11,... | collective-permute-start | bytes 98312 | tf_op jit(solution)/shard_map/ppermute | solution.py:385
  27.4 0.0 copy-done.3
  27.4 0.0 copy-done
  27.4 0.0 copy-done.2
  27.4 0.0 copy-done.1
  27.4 0.0 copy-start.4
  27.4 3.9 %shard_map.86.new_ref = f32[4,8,16,512]{3,2,1,0:T(8,128)S(1)} custom-call(s32[1,128]{1,0:T(1,128)S(1)} %bitcast.2, f32[1,128]{1,0:T(1,128)S(1)} %bitcast.3, f32[4,8,4,4,512]{4,3,2,1,0:T(4,128)S(1)} %copy-done, f32[2,3,8,512]{3,2,1,0:T(8,128)S(1)} %copy-done.3), custom_call_target="tpu_custom_call" | custom-call | flops 4000000000 | bytes 4000000 | tf_op jit(solution)/shard_map/pallas_call | solution.py:416
  31.3 0.0 copy-done.4
  31.3 0.1 copy.9.arrival_ref
  31.4 0.0 collective-permute-done.along_one
  31.4 0.0 collective-permute-done.1.along_two
  31.4 0.0 collective-permute-done.2.cross_one
  31.4 0.0 collective-permute-done.3.cross_two
  31.4 0.0 all-to-all-done.received_ref
  31.4 2.1 %shard_map.88 = (f32[4,8,4,4,512]{4,3,2,1,0:T(4,128)}, f32[8,4,4,512]{3,2,1,0:T(4,128)}) custom-call(s32[8,4]{1,0:T(8,128)S(1)} %copy.9.arrival_ref, f32[4,8,4,4,512]{4,3,2,1,0:T(4,128)S(1)} %copy-done, f32[4,8,16,512]{3,2,1,0:T(8,128)S(1)} %shard_map.86.new_ref, f32[4,16,128]{2,1,0:T(8,128)S(1)} %collective-permute-done.along_one, ...), custom_call_target="tpu_custom_call" | custom-call | flops 10000000 | bytes 4000000 | tf_op jit(solution)/shard_map/pallas_call | solution.py:432
Async XLA Ops:
  0.6 26.8 %copy-start.3 = (f32[2,3,8,512]{3,2,1,0:T(8,128)S(1)}, f32[2,3,8,512]{3,2,1,0:T(8,128)}, u32[]{:S(2)}) copy-start(f32[2,3,8,512]{3,2,1,0:T(8,128)} %constant.2.clone.rows_ref.rows_hbm) | copy-start | bytes 294916
  0.6 26.8 %copy-start = (f32[4,8,4,4,512]{4,3,2,1,0:T(4,128)S(1)}, f32[4,8,4,4,512]{4,3,2,1,0:T(4,128)}, u32[]{:S(2)}) copy-start(f32[4,8,4,4,512]{4,3,2,1,0:T(4,128)} %adj_ref.3) | copy-start | bytes 3145732
  0.7 26.8 %copy-start.2 = (f32[128]{0:T(128)S(1)}, f32[128]{0:T(128)}, u32[]{:S(2)}) copy-start(f32[128]{0:T(128)} %param.12) | copy-start | bytes 1540
  0.7 26.8 %copy-start.1 = (s32[128]{0:T(128)S(1)}, s32[128]{0:T(128)}, u32[]{:S(2)}) copy-start(s32[128]{0:T(128)} %param.11) | copy-start | bytes 1540
  5.9 25.6 %all-to-all-start = ((f32[32,8,512]{2,1,0:T(8,128)}), f32[32,8,512]{2,1,0:T(8,128)S(1)}, u32[]{:S(2)}, u32[]{:S(2)}) async-start(f32[32,8,512]{2,1,0:T(8,128)} %get-tuple-element.11), calls=%async_computation | async-start | bytes 1048576 | tf_op jit(solution)/shard_map/all_to_all | solution.py:411
  16.0 15.4 %collective-permute-start = (f32[4,16,128]{2,1,0:T(8,128)}, f32[4,16,128]{2,1,0:T(8,128)S(1)}, u32[]{:S(2)}, u32[]{:S(2)}) collective-permute-start(f32[4,16,128]{2,1,0:T(8,128)} %get-tuple-element.7), channel_id=1, source_target_pairs={{0,32},{32,0},{64,96},{96,64},{1,33},{33,1},{65,97},{97,65},{2,34}... | collective-permute-start | bytes 98312 | tf_op jit(solution)/shard_map/ppermute | solution.py:385
  17.3 14.1 %collective-permute-start.1 = (f32[4,16,128]{2,1,0:T(8,128)}, f32[4,16,128]{2,1,0:T(8,128)S(1)}, u32[]{:S(2)}, u32[]{:S(2)}) collective-permute-start(f32[4,16,128]{2,1,0:T(8,128)} %get-tuple-element.8), channel_id=1, source_target_pairs={{32,64},{64,32},{33,65},{65,33},{34,66},{66,34},{35,67},{67,35},{3... | collective-permute-start | bytes 98312 | tf_op jit(solution)/shard_map/ppermute | solution.py:385
  19.4 12.0 %collective-permute-start.2 = (f32[4,4,512]{2,1,0:T(4,128)}, f32[4,4,512]{2,1,0:T(4,128)S(1)}, u32[]{:S(2)}, u32[]{:S(2)}) collective-permute-start(f32[4,4,512]{2,1,0:T(4,128)} %get-tuple-element.9), channel_id=1, source_target_pairs={{0,1},{1,0},{2,3},{3,2},{4,5},{5,4},{6,7},{7,6},{8,9},{9,8},{10,11... | collective-permute-start | bytes 98312 | tf_op jit(solution)/shard_map/ppermute | solution.py:385
  20.7 10.7 %collective-permute-start.3 = (f32[4,4,512]{2,1,0:T(4,128)}, f32[4,4,512]{2,1,0:T(4,128)S(1)}, u32[]{:S(2)}, u32[]{:S(2)}) collective-permute-start(f32[4,4,512]{2,1,0:T(4,128)} %get-tuple-element.10), channel_id=1, source_target_pairs={{1,2},{2,1},{3,4},{4,3},{5,6},{6,5},{7,8},{8,7},{9,10},{10,9},{11,... | collective-permute-start | bytes 98312 | tf_op jit(solution)/shard_map/ppermute | solution.py:385
  27.4 3.9 %copy-start.4 = (s32[8,4]{0,1:T(4,128)S(1)}, s32[8,4]{0,1:T(4,128)}, u32[]{:S(2)}) copy-start(s32[8,4]{0,1:T(4,128)} %param.10) | copy-start | bytes 388

commit v3 on v2

--- a/solution.py
+++ b/solution.py
@@ -46,40 +46,50 @@
     matrix = matrix * (1.0 - np.eye(degree + 1))
     matrix[0, 0] = -degree * (degree + 1) / 4.0
     matrix[degree, degree] = degree * (degree + 1) / 4.0
-    twice = 2.0 * matrix.T
-    rows = np.stack(
-        [np.repeat(twice, 64, axis=1), np.tile(np.repeat(twice, 8, axis=1), 8), np.tile(twice, 64)]
-    ).astype(np.float32)
+    twice = 2.0 * matrix
+    half = np.arange(128) // 64
+    along = np.zeros((4, 4, 2, 128))
+    for t in range(4):
+        for source in range(4):
+            along[t, source, 0] = twice[2 * t + half, 2 * source + half]
+            along[t, source, 1] = twice[2 * t + half, 2 * source + 1 - half]
+    rows = np.stack([np.tile(np.repeat(twice.T, 8, axis=1), 2), np.tile(twice.T, 16)]).astype(np.float32)
     high = rows.astype(BF16)
     low = (rows - high.astype(np.float32)).astype(BF16)
-    return np.stack([high, low]).astype(np.float32)
+    parts = [along.reshape(32, 128), *high, *low]
+    return np.concatenate([part.astype(np.float32) for part in parts])
+
+
+def along_slope(x, rows_ref):
+    turned = [pltpu.roll(value, 64, 1) for value in x]
+    slopes = []
+    for t in range(4):
+        slope = None
+        for s in range(4):
+            n = 8 * t + 2 * s
+            term = rows_ref[n : n + 1, :] * x[s] + rows_ref[n + 1 : n + 2, :] * turned[s]
+            slope = term if slope is None else slope + term
+        slopes.append(slope)
+    return slopes
 
 
 def fill_table(rows_ref, table):
     lane = lanes((16, 128))
     sub = lax.broadcasted_iota(jnp.int32, (16, 128), 0)
-    upper = sub >= 8
     zero = jnp.zeros((16, 128), F32)
+    table[...] = jnp.zeros((2, 512, 256), BF16)
     for h in range(2):
-        for i in range(8):
-            for t in range(4):
-                row = rows_ref[h, 0, i : i + 1, tile(t)]
-                for m in range(4):
-                    value = jnp.where((lane & 63) == sub + 16 * m, row, zero)
-                    table[h, 64 * i + 16 * m : 64 * i + 16 * m + 16, tile(t)] = value.astype(BF16)
-        row = rows_ref[h, 2, :, tile(0)]
+        base = 32 + 16 * h
+        row = rows_ref[base + 8 : base + 16, :]
         vertical = jnp.concatenate([row, row], axis=0)
         for g in range(16):
-            here = g // 8
-            j = 2 * g % 8
-            row = jnp.where(upper, rows_ref[h, 1, j + 1 : j + 2, tile(0)], rows_ref[h, 1, j : j + 1, tile(0)])
+            here = tile(g // 8)
+            j = base + 2 * g % 8
+            row = jnp.where(sub >= 8, rows_ref[j + 1 : j + 2, :], rows_ref[j : j + 1, :])
             inside = ((lane >> 6) == g // 4 % 2) & ((lane & 7) == (sub & 7))
-            cross = jnp.where(inside, row, zero).astype(BF16)
+            table[h, 16 * g : 16 * g + 16, here] = jnp.where(inside, row, zero).astype(BF16)
             inside = (lane >> 3) == (sub >> 3) + 2 * (g % 8)
-            level = jnp.where(inside, vertical, zero).astype(BF16)
-            for t in range(2):
-                table[h, 16 * g : 16 * g + 16, tile(4 + t)] = cross if t == here else zero.astype(BF16)
-                table[h, 256 + 16 * g : 272 + 16 * g, tile(4 + t)] = level if t == here else zero.astype(BF16)
+            table[h, 256 + 16 * g : 272 + 16 * g, here] = jnp.where(inside, vertical, zero).astype(BF16)
 
 
 def split(x):
@@ -157,19 +167,20 @@
             slot = slot_ref[4 * g + m]
             for f in range(3):
                 stage[f, g, 4 * m : 4 * m + 4, :] = store_ref[slot, f]
-        for f in range(3):
-            high[f, rows], low[f, rows] = split(stage[f, g])
+        slopes = along_slope([stage[0, g, :, tile(t)] for t in range(4)], rows_ref)
+        for t in range(4):
+            total[pl.ds(2 * g, 2), :, tile(t)] = slopes[t].reshape(2, 8, 128)
+        for f in range(2):
+            high[f, rows], low[f, rows] = split(stage[f + 1, g])
         return carry
 
-    lax.fori_loop(0, 16, gather, 0)
+    lax.fori_loop(0, 16, gather, 0, unroll=16)
     writes = []
     for c in range(2):
         part = slice(256 * c, 256 * c + 256)
-        spread = product(high[0], low[0], table[0, :, part], table[1, :, part])
-        for f in (1, 2):
-            rows = slice(256 * (f - 1), 256 * f)
-            spread += product(high[f, :, part], low[f, :, part], table[0, rows, 512:768], table[1, rows, 512:768])
-        total[:, :, part] = spread.reshape(32, 8, 256)
+        spread = product(high[0, :, part], low[0, :, part], table[0, 0:256], table[1, 0:256])
+        spread += product(high[1, :, part], low[1, :, part], table[0, 256:512], table[1, 256:512])
+        total[:, :, part] += spread.reshape(32, 8, 256)
         writes.append(
             pltpu.make_async_copy(total.at[:, :, part], out_hbm.at[:, :, part], sems.at[7 + c])
         )
@@ -182,8 +193,7 @@
     node_ref, residual_ref, adj_ref, rows_ref, out_ref, table, state, high, low, slope_x, slope_y, slope_z, ground
 ):
     fill_table(rows_ref, table)
-    order = (2, 0, 3, 1)
-    row = {f: 128 * n for n, f in enumerate(order)}
+    row = {2: 0, 0: 128, 3: 256}
     state[:, 0] = jnp.zeros((4, 16, 512), F32)
     state[:, 9] = jnp.zeros((4, 16, 512), F32)
 
@@ -191,19 +201,20 @@
         for f in range(4):
             for c in range(4):
                 state[f, a + 1, 4 * c : 4 * c + 4, :] = adj_ref[f, a, c]
-            rows = pl.ds(pl.multiple_of(row[f] + a * 16, 16), 16)
-            high[rows], low[rows] = split(state[f, a + 1])
+            slopes = along_slope([state[f, a + 1, :, tile(t)] for t in range(4)], rows_ref)
+            for t in range(4):
+                slope_x[f, a, :, tile(t)] = slopes[t]
+            if f in row:
+                rows = pl.ds(pl.multiple_of(row[f] + a * 16, 16), 16)
+                high[rows], low[rows] = split(state[f, a + 1])
         return carry
 
-    lax.fori_loop(0, 8, load, 0)
+    lax.fori_loop(0, 8, load, 0, unroll=8)
     for c in range(2):
         part = slice(256 * c, 256 * c + 256)
-        slope_x[:, part] = product(high[...], low[...], table[0, :, part], table[1, :, part])
-        slope_y[:, part] = product(
-            high[0:256, part], low[0:256, part], table[0, 0:256, 512:768], table[1, 0:256, 512:768]
-        )
+        slope_y[:, part] = product(high[0:256, part], low[0:256, part], table[0, 0:256], table[1, 0:256])
         slope_z[:, part] = product(
-            high[128:384, part], low[128:384, part], table[0, 256:512, 512:768], table[1, 256:512, 512:768]
+            high[128:384, part], low[128:384, part], table[0, 256:512], table[1, 256:512]
         )
 
     node = node_ref[...]
@@ -266,7 +277,7 @@
                 def rows(f, base=0):
                     return pl.ds(pl.multiple_of(row[f] - base + a * 16 + 8 * g, 8), 8)
 
-                gx = [slope_x[rows(f), here] for f in range(4)]
+                gx = [slope_x[f, a, 8 * g : 8 * g + 8, here] for f in range(4)]
                 gy = {f: slope_y[rows(f), here] for f in (2, 0)}
                 gz = {f: slope_z[rows(f, 128), here] for f in (0, 3)}
                 rate = [
@@ -295,12 +306,12 @@
                     out_ref[f, a, 8 * g : 8 * g + 8, here] = new[f]
         return carry
 
-    lax.fori_loop(0, 8, step, 0)
+    lax.fori_loop(0, 8, step, 0, unroll=2)
 
 
 def finish_kernel(
-    arrival_ref, adj_ref, new_ref, along_one, along_two, cross_one, cross_two, received_ref,
-    next_ref, kappa_ref, edge,
+    arrival_ref, adj_ref, new_ref, cross_two, cross_one, along_two, along_one, received_ref,
+    next_hbm, kappa_hbm, next_ref, kappa_ref, edge, side, sems,
 ):
     lift = TIME_STEP * HALF_LIFT
     lane = lanes((4, 128))
@@ -333,19 +344,28 @@
     for t in range(4):
         low = cross_terms(-1.0, t)
         high = cross_terms(1.0, t)
-        for a in range(8):
-            for f in range(4):
+        for f in range(4):
+            side[0, f, :, tile(t)] = low[f]
+            side[1, f, :, tile(t)] = high[f]
+    writes = []
+    for f in range(4):
+        for t in range(4):
+            for a in range(8):
                 for c in range(4):
                     value = new_ref[f, a, 4 * c : 4 * c + 4, tile(t)]
                     if c == 0:
-                        value = value + jnp.where(j == 0, pltpu.roll(low[f], (128 - 8 * a) % 128, 1), 0.0)
+                        beyond = pltpu.roll(side[0, f, :, tile(t)], (128 - 8 * a) % 128, 1)
+                        value = value + jnp.where(j == 0, beyond, 0.0)
                     if c == 3:
-                        value = value + jnp.where(j == 7, pltpu.roll(high[f], (56 - 8 * a) % 128, 1), 0.0)
+                        beyond = pltpu.roll(side[1, f, :, tile(t)], (56 - 8 * a) % 128, 1)
+                        value = value + jnp.where(j == 7, beyond, 0.0)
                     if t == 0 and a == 0:
                         value = value + edge[0, f, 4 * c : 4 * c + 4, :]
                     if t == 3 and a == 7:
                         value = value + edge[1, f, 4 * c : 4 * c + 4, :]
                     next_ref[f, a, c, :, tile(t)] = value
+        writes.append(pltpu.make_async_copy(next_ref.at[f], next_hbm.at[f], sems.at[f]))
+        writes[f].start()
     for a in range(8):
         for c in range(4):
             q = arrival_ref[a, c]
@@ -355,6 +375,10 @@
             block = jnp.where(second, received_ref[holder, 4:8, :], received_ref[holder, 0:4, :])
             value = TIME_STEP * adj_ref[0, a, c] * block
             kappa_ref[a, c] = jnp.where(q >= 0, value, 0.0)
+    writes.append(pltpu.make_async_copy(kappa_ref, kappa_hbm, sems.at[4]))
+    writes[4].start()
+    for write in writes:
+        write.wait()
 
 
 VMEM = pl.BlockSpec(memory_space=pltpu.VMEM)
@@ -394,13 +418,13 @@
         [
             pltpu.SMEM((64,), jnp.int32),
             pltpu.VMEM((64, 3, 4, 512), F32),
-            pltpu.VMEM((2, 3, 8, 512), F32),
-            pltpu.VMEM((2, 512, 768), BF16),
+            pltpu.VMEM((64, 128), F32),
+            pltpu.VMEM((2, 512, 256), BF16),
             pltpu.VMEM((2, 4, 4, 4, 128), F32),
             pltpu.VMEM((2, 4, 8, 4, 512), F32),
             pltpu.VMEM((3, 16, 16, 512), F32),
-            pltpu.VMEM((3, 256, 512), BF16),
-            pltpu.VMEM((3, 256, 512), BF16),
+            pltpu.VMEM((2, 256, 512), BF16),
+            pltpu.VMEM((2, 256, 512), BF16),
             pltpu.VMEM((32, 8, 512), F32),
             pltpu.SemaphoreType.DMA((9,)),
         ],
@@ -418,11 +442,11 @@
         array(4, 8, 16, 512),
         [VMEM] * 4,
         [
-            pltpu.VMEM((2, 512, 768), BF16),
+            pltpu.VMEM((2, 512, 256), BF16),
             pltpu.VMEM((4, 10, 16, 512), F32),
-            pltpu.VMEM((512, 512), BF16),
-            pltpu.VMEM((512, 512), BF16),
-            pltpu.VMEM((512, 512), F32),
+            pltpu.VMEM((384, 512), BF16),
+            pltpu.VMEM((384, 512), BF16),
+            pltpu.VMEM((4, 8, 16, 512), F32),
             pltpu.VMEM((256, 512), F32),
             pltpu.VMEM((256, 512), F32),
             pltpu.VMEM((128, 512), F32),
@@ -433,10 +457,17 @@
         finish_kernel,
         (array(4, 8, 4, 4, 512), array(8, 4, 4, 512)),
         [SMEM] + [VMEM] * 7,
-        [pltpu.VMEM((2, 4, 16, 128), F32)],
+        [
+            pltpu.VMEM((4, 8, 4, 4, 512), F32),
+            pltpu.VMEM((8, 4, 4, 512), F32),
+            pltpu.VMEM((2, 4, 16, 128), F32),
+            pltpu.VMEM((2, 4, 4, 512), F32),
+            pltpu.SemaphoreType.DMA((5,)),
+        ],
         10_000_000, 4_000_000,
+        (HBM, HBM),
     )(
-        arrival_slot, adjoint_state, updated, along_one, along_two, cross_one, cross_two, received
+        arrival_slot, adjoint_state, updated, cross_two, cross_one, along_two, along_one, received
     )
 
 

time: 33.8 us -> 31.2 us (0.923)
  the two profiles are of different devices: /device:TPU:33 before, /device:TPU:0 now
where the time goes in v3:
time: 31.2 us; the launch traced here: 30.9 us
  starting transfers between devices  18.8 us (60%)
  Pallas kernels  8.89 us (28%)
  waiting for transfers between devices  2.37 us (8%)
  between operations  0.74 us (2%)
    all_to_all x1, starting transfers between devices, per_device(): lax.all_to_all(outgoing, 'cross', split_axis=0, concat_axis=0, tiled=True)  10.9 us
    ppermute x4, starting transfers between devices, exchange(): return lax.ppermute(value, axis, pairs)  7.92 us
    pallas_call x1, Pallas kernels, per_device(): kernel(holder_kernel, (array(32, 8, 512), array(4, 16, 128), array(4, 16,...  4.33 us
    pallas_call x1, Pallas kernels, per_device(): kernel(volume_kernel, array(4, 8, 16, 512), [VMEM] * 4, [pltpu.VMEM((2, 5...  2.68 us
    all_to_all x1, waiting for transfers between devices, per_device(): lax.all_to_all(outgoing, 'cross', split_axis=0, concat_axis=0, tiled=True)  2.36 us
    pallas_call x1, Pallas kernels, per_device(): kernel(finish_kernel, (array(4, 8, 4, 4, 512), array(8, 4, 4, 512)), [SME...  1.88 us
  transfers between devices with their start and end apart: 5, of which 1 were waited for; matrix products, arithmetic and copies ran while one was open for 0% of the time, Pallas kernels for 9%

profile of v3, /device:TPU:0, one launch (start us, length us, event | category | flops | bytes accessed | tf_op | source)
XLA Modules:
  0.0 30.9 jit_solution(1180605122020045554)
XLA Ops:
  0.6 0.0 copy-start.3
  0.6 0.0 copy-start
  0.7 0.0 copy-start.2
  0.7 0.0 copy-start.1
  0.7 4.3 %shard_map.87 = (f32[32,8,512]{2,1,0:T(8,128)}, f32[4,16,128]{2,1,0:T(8,128)}, f32[4,16,128]{2,1,0:T(8,128)}, f32[4,4,512]{2,1,0:T(4,128)}, f32[4,4,512]{2,1,0:T(4,128)}) custom-call(s32[64]{0:T(128)} %slot_hbm.1, f32[4,8,4,4,512]{4,3,2,1,0:T(4,128)} %adj_ref.3, f32[64,3,4,512]{3,2,1,0:T(4,128)} %store_hbm.1, f32[64,128]{1,0:T(8,128)} %constant.2.clone.rows_ref.rows_hbm), custom_call_target="tpu_custom_call" | custom-call | flops 3000000000 | bytes 5000000 | tf_op jit(solution)/shard_map/pallas_call | solution.py:414
  5.0 10.9 %all-to-all-start = ((f32[32,8,512]{2,1,0:T(8,128)}), f32[32,8,512]{2,1,0:T(8,128)S(1)}, u32[]{:S(2)}, u32[]{:S(2)}) async-start(f32[32,8,512]{2,1,0:T(8,128)} %get-tuple-element.11), calls=%async_computation | async-start | bytes 1048576 | tf_op jit(solution)/shard_map/all_to_all | solution.py:435
  15.9 0.7 %collective-permute-start = (f32[4,4,512]{2,1,0:T(4,128)}, f32[4,4,512]{2,1,0:T(4,128)S(1)}, u32[]{:S(2)}, u32[]{:S(2)}) collective-permute-start(f32[4,4,512]{2,1,0:T(4,128)} %get-tuple-element.7), channel_id=1, source_target_pairs={{1,2},{2,1},{3,4},{4,3},{5,6},{6,5},{7,8},{8,7},{9,10},{10,9},{11,... | collective-permute-start | bytes 98312 | tf_op jit(solution)/shard_map/ppermute | solution.py:409
  16.6 4.6 %collective-permute-start.1 = (f32[4,4,512]{2,1,0:T(4,128)}, f32[4,4,512]{2,1,0:T(4,128)S(1)}, u32[]{:S(2)}, u32[]{:S(2)}) collective-permute-start(f32[4,4,512]{2,1,0:T(4,128)} %get-tuple-element.8), channel_id=1, source_target_pairs={{0,1},{1,0},{2,3},{3,2},{4,5},{5,4},{6,7},{7,6},{8,9},{9,8},{10,11... | collective-permute-start | bytes 98312 | tf_op jit(solution)/shard_map/ppermute | solution.py:409
  21.2 0.7 %collective-permute-start.2 = (f32[4,16,128]{2,1,0:T(8,128)}, f32[4,16,128]{2,1,0:T(8,128)S(1)}, u32[]{:S(2)}, u32[]{:S(2)}) collective-permute-start(f32[4,16,128]{2,1,0:T(8,128)} %get-tuple-element.9), channel_id=1, source_target_pairs={{32,64},{64,32},{33,65},{65,33},{34,66},{66,34},{35,67},{67,35},{3... | collective-permute-start | bytes 98312 | tf_op jit(solution)/shard_map/ppermute | solution.py:409
  21.8 2.0 %collective-permute-start.3 = (f32[4,16,128]{2,1,0:T(8,128)}, f32[4,16,128]{2,1,0:T(8,128)S(1)}, u32[]{:S(2)}, u32[]{:S(2)}) collective-permute-start(f32[4,16,128]{2,1,0:T(8,128)} %get-tuple-element.10), channel_id=1, source_target_pairs={{0,32},{32,0},{64,96},{96,64},{1,33},{33,1},{65,97},{97,65},{2,34}... | collective-permute-start | bytes 98312 | tf_op jit(solution)/shard_map/ppermute | solution.py:409
  23.8 0.0 copy-done.3
  23.8 0.0 copy-done
  23.8 0.0 copy-done.2
  23.8 0.0 copy-done.1
  23.9 0.0 copy-start.4
  23.9 2.7 %shard_map.86.new_ref = f32[4,8,16,512]{3,2,1,0:T(8,128)S(1)} custom-call(s32[1,128]{1,0:T(1,128)S(1)} %bitcast.2, f32[1,128]{1,0:T(1,128)S(1)} %bitcast.3, f32[4,8,4,4,512]{4,3,2,1,0:T(4,128)S(1)} %copy-done, f32[64,128]{1,0:T(8,128)S(1)} %copy-done.3), custom_call_target="tpu_custom_call" | custom-call | flops 4000000000 | bytes 4000000 | tf_op jit(solution)/shard_map/pallas_call | solution.py:440
  26.6 0.0 copy-done.4
  26.6 0.1 copy.9.arrival_ref
  26.6 0.0 collective-permute-done.cross_two
  26.7 0.0 collective-permute-done.1.cross_one
  26.7 0.0 collective-permute-done.2.along_two
  26.7 0.0 collective-permute-done.3.along_one
  26.7 2.4 %all-to-all-done.received_ref = f32[32,8,512]{2,1,0:T(8,128)S(1)} async-done(((f32[32,8,512]{2,1,0:T(8,128)}), f32[32,8,512]{2,1,0:T(8,128)S(1)}, u32[]{:S(2)}, u32[]{:S(2)}) %all-to-all-start) | async-done | bytes 524320 | tf_op jit(solution)/shard_map/all_to_all | solution.py:435
  29.0 1.9 %shard_map.88 = (f32[4,8,4,4,512]{4,3,2,1,0:T(4,128)}, f32[8,4,4,512]{3,2,1,0:T(4,128)}) custom-call(s32[8,4]{1,0:T(8,128)S(1)} %copy.9.arrival_ref, f32[4,8,4,4,512]{4,3,2,1,0:T(4,128)S(1)} %copy-done, f32[4,8,16,512]{3,2,1,0:T(8,128)S(1)} %shard_map.86.new_ref, f32[4,4,512]{2,1,0:T(4,128)S(1)} %collective-permute-done.cross_two, ...), custom_call_target="tpu_custom_call" | custom-call | flops 10000000 | bytes 4000000 | tf_op jit(solution)/shard_map/pallas_call | solution.py:456
Async XLA Ops:
  0.6 23.2 %copy-start.3 = (f32[64,128]{1,0:T(8,128)S(1)}, f32[64,128]{1,0:T(8,128)}, u32[]{:S(2)}) copy-start(f32[64,128]{1,0:T(8,128)} %constant.2.clone.rows_ref.rows_hbm) | copy-start | bytes 98308
  0.6 23.2 %copy-start = (f32[4,8,4,4,512]{4,3,2,1,0:T(4,128)S(1)}, f32[4,8,4,4,512]{4,3,2,1,0:T(4,128)}, u32[]{:S(2)}) copy-start(f32[4,8,4,4,512]{4,3,2,1,0:T(4,128)} %adj_ref.3) | copy-start | bytes 3145732
  0.7 23.2 %copy-start.2 = (f32[128]{0:T(128)S(1)}, f32[128]{0:T(128)}, u32[]{:S(2)}) copy-start(f32[128]{0:T(128)} %param.12) | copy-start | bytes 1540
  0.7 23.2 %copy-start.1 = (s32[128]{0:T(128)S(1)}, s32[128]{0:T(128)}, u32[]{:S(2)}) copy-start(s32[128]{0:T(128)} %param.11) | copy-start | bytes 1540
  5.0 24.0 %all-to-all-start = ((f32[32,8,512]{2,1,0:T(8,128)}), f32[32,8,512]{2,1,0:T(8,128)S(1)}, u32[]{:S(2)}, u32[]{:S(2)}) async-start(f32[32,8,512]{2,1,0:T(8,128)} %get-tuple-element.11), calls=%async_computation | async-start | bytes 1048576 | tf_op jit(solution)/shard_map/all_to_all | solution.py:435
  15.9 10.7 %collective-permute-start = (f32[4,4,512]{2,1,0:T(4,128)}, f32[4,4,512]{2,1,0:T(4,128)S(1)}, u32[]{:S(2)}, u32[]{:S(2)}) collective-permute-start(f32[4,4,512]{2,1,0:T(4,128)} %get-tuple-element.7), channel_id=1, source_target_pairs={{1,2},{2,1},{3,4},{4,3},{5,6},{6,5},{7,8},{8,7},{9,10},{10,9},{11,... | collective-permute-start | bytes 98312 | tf_op jit(solution)/shard_map/ppermute | solution.py:409
  16.6 10.1 %collective-permute-start.1 = (f32[4,4,512]{2,1,0:T(4,128)}, f32[4,4,512]{2,1,0:T(4,128)S(1)}, u32[]{:S(2)}, u32[]{:S(2)}) collective-permute-start(f32[4,4,512]{2,1,0:T(4,128)} %get-tuple-element.8), channel_id=1, source_target_pairs={{0,1},{1,0},{2,3},{3,2},{4,5},{5,4},{6,7},{7,6},{8,9},{9,8},{10,11... | collective-permute-start | bytes 98312 | tf_op jit(solution)/shard_map/ppermute | solution.py:409
  21.2 5.5 %collective-permute-start.2 = (f32[4,16,128]{2,1,0:T(8,128)}, f32[4,16,128]{2,1,0:T(8,128)S(1)}, u32[]{:S(2)}, u32[]{:S(2)}) collective-permute-start(f32[4,16,128]{2,1,0:T(8,128)} %get-tuple-element.9), channel_id=1, source_target_pairs={{32,64},{64,32},{33,65},{65,33},{34,66},{66,34},{35,67},{67,35},{3... | collective-permute-start | bytes 98312 | tf_op jit(solution)/shard_map/ppermute | solution.py:409
  21.8 4.9 %collective-permute-start.3 = (f32[4,16,128]{2,1,0:T(8,128)}, f32[4,16,128]{2,1,0:T(8,128)S(1)}, u32[]{:S(2)}, u32[]{:S(2)}) collective-permute-start(f32[4,16,128]{2,1,0:T(8,128)} %get-tuple-element.10), channel_id=1, source_target_pairs={{0,32},{32,0},{64,96},{96,64},{1,33},{33,1},{65,97},{97,65},{2,34}... | collective-permute-start | bytes 98312 | tf_op jit(solution)/shard_map/ppermute | solution.py:409
  23.9 2.7 %copy-start.4 = (s32[8,4]{0,1:T(4,128)S(1)}, s32[8,4]{0,1:T(4,128)}, u32[]{:S(2)}) copy-start(s32[8,4]{0,1:T(4,128)} %param.10) | copy-start | bytes 388

commit v4 on v3

--- a/solution.py
+++ b/solution.py
@@ -117,46 +117,19 @@
 
 
 def holder_kernel(
-    slot_hbm, adj_hbm, store_hbm, rows_hbm,
-    out_hbm, along_one, along_two, cross_one, cross_two,
-    slot_ref, store_ref, rows_ref, table, face_along, face_cross, stage, high, low, total, sems,
+    slot_hbm, store_hbm, rows_hbm,
+    out_hbm,
+    slot_ref, store_ref, rows_ref, table, stage, high, low, total, sems,
 ):
     pieces = [
         (slot_hbm, slot_ref),
         (store_hbm, store_ref),
-        (adj_hbm.at[:, 0, :, :, tile(0)], face_along.at[0]),
-        (adj_hbm.at[:, 7, :, :, tile(3)], face_along.at[1]),
-        (adj_hbm.at[:, :, 0], face_cross.at[0]),
-        (adj_hbm.at[:, :, 3], face_cross.at[1]),
         (rows_hbm, rows_ref),
     ]
     copies = [pltpu.make_async_copy(src, dst, sems.at[n]) for n, (src, dst) in enumerate(pieces)]
     for copy in copies:
         copy.start()
-    for n in (2, 3, 4, 5):
-        copies[n].wait()
-    even = is_even("along")
-    for f in range(4):
-        for c in range(4):
-            rows = slice(4 * c, 4 * c + 4)
-            first = face_along[0, f, c]
-            last = face_along[1, f, c]
-            along_one[f, rows, :] = jnp.where(even, last, first)
-            along_two[f, rows, :] = jnp.where(even, first, last)
-    even = is_even("cross")
-    j = (lanes((4, 128)) >> 3) & 7
-    for f in range(4):
-        for t in range(4):
-            last = pltpu.roll(face_cross[1, f, 0, :, tile(t)], 72, 1)
-            first = face_cross[0, f, 0, :, tile(t)]
-            for a in range(1, 8):
-                other = face_cross[1, f, a, :, tile(t)]
-                last = jnp.where(j == a, pltpu.roll(other, (72 + 8 * a) % 128, 1), last)
-                other = face_cross[0, f, a, :, tile(t)]
-                first = jnp.where(j == a, pltpu.roll(other, 8 * a, 1), first)
-            cross_one[f, :, tile(t)] = jnp.where(even, last, first)
-            cross_two[f, :, tile(t)] = jnp.where(even, first, last)
-    copies[6].wait()
+    copies[2].wait()
     fill_table(rows_ref, table)
     copies[0].wait()
     copies[1].wait()
@@ -182,11 +155,35 @@
         spread += product(high[1, :, part], low[1, :, part], table[0, 256:512], table[1, 256:512])
         total[:, :, part] += spread.reshape(32, 8, 256)
         writes.append(
-            pltpu.make_async_copy(total.at[:, :, part], out_hbm.at[:, :, part], sems.at[7 + c])
+            pltpu.make_async_copy(total.at[:, :, part], out_hbm.at[:, :, part], sems.at[3 + c])
         )
         writes[c].start()
     for write in writes:
         write.wait()
+
+
+def trace_kernel(adj_ref, along_one, along_two, cross_one, cross_two):
+    even = is_even("along")
+    for f in range(4):
+        for c in range(4):
+            rows = slice(4 * c, 4 * c + 4)
+            first = adj_ref[f, 0, c, :, tile(0)]
+            last = adj_ref[f, 7, c, :, tile(3)]
+            along_one[f, rows, :] = jnp.where(even, last, first)
+            along_two[f, rows, :] = jnp.where(even, first, last)
+    even = is_even("cross")
+    j = (lanes((4, 128)) >> 3) & 7
+    for f in range(4):
+        for t in range(4):
+            last = pltpu.roll(adj_ref[f, 0, 3, :, tile(t)], 72, 1)
+            first = adj_ref[f, 0, 0, :, tile(t)]
+            for a in range(1, 8):
+                other = adj_ref[f, a, 3, :, tile(t)]
+                last = jnp.where(j == a, pltpu.roll(other, (72 + 8 * a) % 128, 1), last)
+                other = adj_ref[f, a, 0, :, tile(t)]
+                first = jnp.where(j == a, pltpu.roll(other, 8 * a, 1), first)
+            cross_one[f, :, tile(t)] = jnp.where(even, last, first)
+            cross_two[f, :, tile(t)] = jnp.where(even, first, last)
 
 
 def volume_kernel(
@@ -411,32 +408,33 @@
 
 def per_device(adjoint_state, snapshot_store, dispatch_slot, arrival_slot, mic_node, mic_residual):
     rows = jnp.asarray(derivative_rows())
-    outgoing, along_one, along_two, cross_one, cross_two = kernel(
+    outgoing = kernel(
         holder_kernel,
-        (array(32, 8, 512), array(4, 16, 128), array(4, 16, 128), array(4, 4, 512), array(4, 4, 512)),
-        [HBM] * 4,
+        array(32, 8, 512),
+        [HBM] * 3,
         [
             pltpu.SMEM((64,), jnp.int32),
             pltpu.VMEM((64, 3, 4, 512), F32),
             pltpu.VMEM((64, 128), F32),
             pltpu.VMEM((2, 512, 256), BF16),
-            pltpu.VMEM((2, 4, 4, 4, 128), F32),
-            pltpu.VMEM((2, 4, 8, 4, 512), F32),
             pltpu.VMEM((3, 16, 16, 512), F32),
             pltpu.VMEM((2, 256, 512), BF16),
             pltpu.VMEM((2, 256, 512), BF16),
             pltpu.VMEM((32, 8, 512), F32),
-            pltpu.SemaphoreType.DMA((9,)),
+            pltpu.SemaphoreType.DMA((5,)),
         ],
         3_000_000_000, 5_000_000,
-        (HBM, VMEM, VMEM, VMEM, VMEM),
+        HBM,
         HOLDER_BYTES,
-    )(dispatch_slot, adjoint_state, snapshot_store, rows)
+    )(dispatch_slot, snapshot_store, rows)
     received = lax.all_to_all(outgoing, "cross", split_axis=0, concat_axis=0, tiled=True)
-    along_one = exchange(along_one, "along", 0)
-    along_two = exchange(along_two, "along", 1)
-    cross_one = exchange(cross_one, "cross", 0)
-    cross_two = exchange(cross_two, "cross", 1)
+    along_one, along_two, cross_one, cross_two = kernel(
+        trace_kernel,
+        (array(4, 16, 128), array(4, 16, 128), array(4, 4, 512), array(4, 4, 512)),
+        [VMEM],
+        [],
+        1_000_000, 500_000,
+    )(adjoint_state)
     updated = kernel(
         volume_kernel,
         array(4, 8, 16, 512),
@@ -453,6 +451,10 @@
         ],
         4_000_000_000, 4_000_000,
     )(mic_node.reshape(1, 128), mic_residual.reshape(1, 128), adjoint_state, rows)
+    along_one = exchange(along_one, "along", 0)
+    along_two = exchange(along_two, "along", 1)
+    cross_one = exchange(cross_one, "cross", 0)
+    cross_two = exchange(cross_two, "cross", 1)
     return kernel(
         finish_kernel,
         (array(4, 8, 4, 4, 512), array(8, 4, 4, 512)),

time: 31.2 us -> 30.3 us (0.971)
  the two profiles are of different devices: /device:TPU:0 before, /device:TPU:41 now
where the time goes in v4:
time: 30.3 us; the launch traced here: 30 us
  starting transfers between devices  21.2 us (70%)
  Pallas kernels  7.94 us (26%)
  between operations  0.79 us (3%)
    ppermute x4, starting transfers between devices, exchange(): return lax.ppermute(value, axis, pairs)  11 us
    all_to_all x1, starting transfers between devices, per_device(): lax.all_to_all(outgoing, 'cross', split_axis=0, concat_axis=0, tiled=True)  10.1 us
    pallas_call x1, Pallas kernels, per_device(): kernel(holder_kernel, array(32, 8, 512), [HBM] * 3, [pltpu.SMEM((64,), jn...  3.06 us
    pallas_call x1, Pallas kernels, per_device(): kernel(volume_kernel, array(4, 8, 16, 512), [VMEM] * 4, [pltpu.VMEM((2, 5...  2.7 us
    pallas_call x1, Pallas kernels, per_device(): kernel(finish_kernel, (array(4, 8, 4, 4, 512), array(8, 4, 4, 512)), [SME...  1.88 us
  transfers between devices with their start and end apart: 5, of which 0 were waited for; matrix products, arithmetic and copies ran while one was open for 0% of the time, Pallas kernels for 10%

profile of v4, /device:TPU:41, one launch (start us, length us, event | category | flops | bytes accessed | tf_op | source)
XLA Modules:
  0.0 30.0 jit_solution(16888305232371368552)
XLA Ops:
  0.6 3.1 %shard_map.88 = f32[32,8,512]{2,1,0:T(8,128)} custom-call(s32[64]{0:T(128)} %slot_hbm.1, f32[64,3,4,512]{3,2,1,0:T(4,128)} %store_hbm.1, f32[64,128]{1,0:T(8,128)} %constant.2.clone.rows_ref.rows_hbm), custom_call_target="tpu_custom_call" | custom-call | flops 3000000000 | bytes 5000000 | tf_op jit(solution)/shard_map/pallas_call | solution.py:411
  3.7 0.0 copy-start
  3.7 0.0 copy-start.1
  3.7 0.0 copy-start.2
  3.7 0.0 copy-start.3
  3.7 10.1 %all-to-all-start = ((f32[32,8,512]{2,1,0:T(8,128)}), f32[32,8,512]{2,1,0:T(8,128)S(1)}, u32[]{:S(2)}, u32[]{:S(2)}) async-start(f32[32,8,512]{2,1,0:T(8,128)} %shard_map.88), calls=%async_computation | async-start | bytes 1048576 | tf_op jit(solution)/shard_map/all_to_all | solution.py:430
  13.9 0.0 copy-done
  13.9 0.3 shard_map.87
  14.2 3.1 %collective-permute-start = (f32[4,4,512]{2,1,0:T(4,128)S(1)}, f32[4,4,512]{2,1,0:T(4,128)S(1)}, u32[]{:S(2)}, u32[]{:S(2)}) collective-permute-start(f32[4,4,512]{2,1,0:T(4,128)S(1)} %get-tuple-element.6), channel_id=1, source_target_pairs={{1,2},{2,1},{3,4},{4,3},{5,6},{6,5},{7,8},{8,7},{9,10},{10,9},{11,... | collective-permute-start | bytes 98312 | tf_op jit(solution)/shard_map/ppermute | solution.py:406
  17.3 4.0 %collective-permute-start.1 = (f32[4,4,512]{2,1,0:T(4,128)S(1)}, f32[4,4,512]{2,1,0:T(4,128)S(1)}, u32[]{:S(2)}, u32[]{:S(2)}) collective-permute-start(f32[4,4,512]{2,1,0:T(4,128)S(1)} %get-tuple-element.7), channel_id=1, source_target_pairs={{0,1},{1,0},{2,3},{3,2},{4,5},{5,4},{6,7},{7,6},{8,9},{9,8},{10,11... | collective-permute-start | bytes 98312 | tf_op jit(solution)/shard_map/ppermute | solution.py:406
  21.3 3.9 %collective-permute-start.2 = (f32[4,16,128]{2,1,0:T(8,128)S(1)}, f32[4,16,128]{2,1,0:T(8,128)S(1)}, u32[]{:S(2)}, u32[]{:S(2)}) collective-permute-start(f32[4,16,128]{2,1,0:T(8,128)S(1)} %get-tuple-element.8), channel_id=1, source_target_pairs={{32,64},{64,32},{33,65},{65,33},{34,66},{66,34},{35,67},{67,35},{3... | collective-permute-start | bytes 98312 | tf_op jit(solution)/shard_map/ppermute | solution.py:406
  25.2 0.1 collective-permute-start.3
  25.3 0.0 copy-done.1
  25.3 0.0 copy-done.2
  25.3 0.0 copy-done.3
  25.3 0.0 copy-start.4
  25.3 2.7 %shard_map.86.new_ref = f32[4,8,16,512]{3,2,1,0:T(8,128)S(1)} custom-call(s32[1,128]{1,0:T(1,128)S(1)} %bitcast.2, f32[1,128]{1,0:T(1,128)S(1)} %bitcast.3, f32[4,8,4,4,512]{4,3,2,1,0:T(4,128)S(1)} %copy-done, f32[64,128]{1,0:T(8,128)S(1)} %copy-done.3), custom_call_target="tpu_custom_call" | custom-call | flops 4000000000 | bytes 4000000 | tf_op jit(solution)/shard_map/pallas_call | solution.py:438
  28.0 0.1 copy.9.arrival_ref
  28.1 0.0 collective-permute-done.cross_two
  28.1 0.0 collective-permute-done.1.cross_one
  28.1 0.0 collective-permute-done.2.along_two
  28.1 0.0 collective-permute-done.3.along_one
  28.1 0.0 all-to-all-done.received_ref
  28.1 1.9 %shard_map.89 = (f32[4,8,4,4,512]{4,3,2,1,0:T(4,128)}, f32[8,4,4,512]{3,2,1,0:T(4,128)}) custom-call(s32[8,4]{1,0:T(8,128)S(1)} %copy.9.arrival_ref, f32[4,8,4,4,512]{4,3,2,1,0:T(4,128)S(1)} %copy-done, f32[4,8,16,512]{3,2,1,0:T(8,128)S(1)} %shard_map.86.new_ref, f32[4,4,512]{2,1,0:T(4,128)S(1)} %collective-permute-done.cross_two, ...), custom_call_target="tpu_custom_call" | custom-call | flops 10000000 | bytes 4000000 | tf_op jit(solution)/shard_map/pallas_call | solution.py:458
  (1 shorter events, 0.0 us)
Async XLA Ops:
  3.7 10.2 %copy-start = (f32[4,8,4,4,512]{4,3,2,1,0:T(4,128)S(1)}, f32[4,8,4,4,512]{4,3,2,1,0:T(4,128)}, u32[]{:S(2)}) copy-start(f32[4,8,4,4,512]{4,3,2,1,0:T(4,128)} %adj_ref.5) | copy-start | bytes 3145732
  3.7 21.6 %copy-start.1 = (s32[128]{0:T(128)S(1)}, s32[128]{0:T(128)}, u32[]{:S(2)}) copy-start(s32[128]{0:T(128)} %param.11) | copy-start | bytes 1540
  3.7 21.6 %copy-start.2 = (f32[128]{0:T(128)S(1)}, f32[128]{0:T(128)}, u32[]{:S(2)}) copy-start(f32[128]{0:T(128)} %param.12) | copy-start | bytes 1540
  3.7 21.6 %copy-start.3 = (f32[64,128]{1,0:T(8,128)S(1)}, f32[64,128]{1,0:T(8,128)}, u32[]{:S(2)}) copy-start(f32[64,128]{1,0:T(8,128)} %constant.2.clone.rows_ref.rows_hbm) | copy-start | bytes 98308
  3.7 24.4 %all-to-all-start = ((f32[32,8,512]{2,1,0:T(8,128)}), f32[32,8,512]{2,1,0:T(8,128)S(1)}, u32[]{:S(2)}, u32[]{:S(2)}) async-start(f32[32,8,512]{2,1,0:T(8,128)} %shard_map.88), calls=%async_computation | async-start | bytes 1048576 | tf_op jit(solution)/shard_map/all_to_all | solution.py:430
  14.2 13.9 %collective-permute-start = (f32[4,4,512]{2,1,0:T(4,128)S(1)}, f32[4,4,512]{2,1,0:T(4,128)S(1)}, u32[]{:S(2)}, u32[]{:S(2)}) collective-permute-start(f32[4,4,512]{2,1,0:T(4,128)S(1)} %get-tuple-element.6), channel_id=1, source_target_pairs={{1,2},{2,1},{3,4},{4,3},{5,6},{6,5},{7,8},{8,7},{9,10},{10,9},{11,... | collective-permute-start | bytes 98312 | tf_op jit(solution)/shard_map/ppermute | solution.py:406
  17.3 10.8 %collective-permute-start.1 = (f32[4,4,512]{2,1,0:T(4,128)S(1)}, f32[4,4,512]{2,1,0:T(4,128)S(1)}, u32[]{:S(2)}, u32[]{:S(2)}) collective-permute-start(f32[4,4,512]{2,1,0:T(4,128)S(1)} %get-tuple-element.7), channel_id=1, source_target_pairs={{0,1},{1,0},{2,3},{3,2},{4,5},{5,4},{6,7},{7,6},{8,9},{9,8},{10,11... | collective-permute-start | bytes 98312 | tf_op jit(solution)/shard_map/ppermute | solution.py:406
  21.3 6.8 %collective-permute-start.2 = (f32[4,16,128]{2,1,0:T(8,128)S(1)}, f32[4,16,128]{2,1,0:T(8,128)S(1)}, u32[]{:S(2)}, u32[]{:S(2)}) collective-permute-start(f32[4,16,128]{2,1,0:T(8,128)S(1)} %get-tuple-element.8), channel_id=1, source_target_pairs={{32,64},{64,32},{33,65},{65,33},{34,66},{66,34},{35,67},{67,35},{3... | collective-permute-start | bytes 98312 | tf_op jit(solution)/shard_map/ppermute | solution.py:406
  25.2 2.9 %collective-permute-start.3 = (f32[4,16,128]{2,1,0:T(8,128)S(1)}, f32[4,16,128]{2,1,0:T(8,128)S(1)}, u32[]{:S(2)}, u32[]{:S(2)}) collective-permute-start(f32[4,16,128]{2,1,0:T(8,128)S(1)} %get-tuple-element.9), channel_id=1, source_target_pairs={{0,32},{32,0},{64,96},{96,64},{1,33},{33,1},{65,97},{97,65},{2,34}... | collective-permute-start | bytes 98312 | tf_op jit(solution)/shard_map/ppermute | solution.py:406
  25.3 2.7 %copy-start.4 = (s32[8,4]{0,1:T(4,128)S(1)}, s32[8,4]{0,1:T(4,128)}, u32[]{:S(2)}) copy-start(s32[8,4]{0,1:T(4,128)} %param.10) | copy-start | bytes 388

commit v5 on v4

--- a/solution.py
+++ b/solution.py
@@ -303,11 +303,11 @@
                     out_ref[f, a, 8 * g : 8 * g + 8, here] = new[f]
         return carry
 
-    lax.fori_loop(0, 8, step, 0, unroll=2)
+    lax.fori_loop(0, 8, step, 0, unroll=8)
 
 
 def finish_kernel(
-    arrival_ref, adj_ref, new_ref, cross_two, cross_one, along_two, along_one, received_ref,
+    arrival_ref, adj_ref, new_ref, cross_two, along_two, cross_one, along_one, received_ref,
     next_hbm, kappa_hbm, next_ref, kappa_ref, edge, side, sems,
 ):
     lift = TIME_STEP * HALF_LIFT
@@ -469,7 +469,7 @@
         10_000_000, 4_000_000,
         (HBM, HBM),
     )(
-        arrival_slot, adjoint_state, updated, cross_two, cross_one, along_two, along_one, received
+        arrival_slot, adjoint_state, updated, cross_two, along_two, cross_one, along_one, received
     )
 
 

time: 30.3 us -> 30 us (0.990)
  the two profiles are of different devices: /device:TPU:41 before, /device:TPU:0 now
where the time goes in v5:
time: 30 us; the launch traced here: 29.8 us
  starting transfers between devices  18.6 us (62%)
  Pallas kernels  7.47 us (25%)
  waiting for transfers between devices  2.86 us (10%)
  between operations  0.74 us (2%)
    all_to_all x1, starting transfers between devices, per_device(): lax.all_to_all(outgoing, 'cross', split_axis=0, concat_axis=0, tiled=True)  11 us
    ppermute x4, starting transfers between devices, exchange(): return lax.ppermute(value, axis, pairs)  7.58 us
    pallas_call x1, Pallas kernels, per_device(): kernel(holder_kernel, array(32, 8, 512), [HBM] * 3, [pltpu.SMEM((64,), jn...  3.06 us
    all_to_all x1, waiting for transfers between devices, per_device(): lax.all_to_all(outgoing, 'cross', split_axis=0, concat_axis=0, tiled=True)  2.85 us
    pallas_call x1, Pallas kernels, per_device(): kernel(volume_kernel, array(4, 8, 16, 512), [VMEM] * 4, [pltpu.VMEM((2, 5...  2.23 us
    pallas_call x1, Pallas kernels, per_device(): kernel(finish_kernel, (array(4, 8, 4, 4, 512), array(8, 4, 4, 512)), [SME...  1.88 us
  transfers between devices with their start and end apart: 5, of which 1 were waited for; matrix products, arithmetic and copies ran while one was open for 0% of the time, Pallas kernels for 8%

profile of v5, /device:TPU:0, one launch (start us, length us, event | category | flops | bytes accessed | tf_op | source)
XLA Modules:
  0.0 29.8 jit_solution(10221279446137760199)
XLA Ops:
  0.6 3.1 %shard_map.88 = f32[32,8,512]{2,1,0:T(8,128)} custom-call(s32[64]{0:T(128)} %slot_hbm.1, f32[64,3,4,512]{3,2,1,0:T(4,128)} %store_hbm.1, f32[64,128]{1,0:T(8,128)} %constant.2.clone.rows_ref.rows_hbm), custom_call_target="tpu_custom_call" | custom-call | flops 3000000000 | bytes 5000000 | tf_op jit(solution)/shard_map/pallas_call | solution.py:411
  3.7 0.0 copy-start
  3.7 0.0 copy-start.1
  3.7 0.0 copy-start.2
  3.7 0.0 copy-start.3
  3.7 11.0 %all-to-all-start = ((f32[32,8,512]{2,1,0:T(8,128)}), f32[32,8,512]{2,1,0:T(8,128)S(1)}, u32[]{:S(2)}, u32[]{:S(2)}) async-start(f32[32,8,512]{2,1,0:T(8,128)} %shard_map.88), calls=%async_computation | async-start | bytes 1048576 | tf_op jit(solution)/shard_map/all_to_all | solution.py:430
  14.8 0.0 copy-done
  14.8 0.3 %shard_map.87 = (f32[4,16,128]{2,1,0:T(8,128)S(1)}, f32[4,16,128]{2,1,0:T(8,128)S(1)}, f32[4,4,512]{2,1,0:T(4,128)S(1)}, f32[4,4,512]{2,1,0:T(4,128)S(1)}) custom-call(f32[4,8,4,4,512]{4,3,2,1,0:T(4,128)S(1)} %copy-done), custom_call_target="tpu_custom_call" | custom-call | flops 1000000 | bytes 500000 | tf_op jit(solution)/shard_map/pallas_call | solution.py:431
  15.1 0.7 %collective-permute-start = (f32[4,4,512]{2,1,0:T(4,128)S(1)}, f32[4,4,512]{2,1,0:T(4,128)S(1)}, u32[]{:S(2)}, u32[]{:S(2)}) collective-permute-start(f32[4,4,512]{2,1,0:T(4,128)S(1)} %get-tuple-element.6), channel_id=1, source_target_pairs={{1,2},{2,1},{3,4},{4,3},{5,6},{6,5},{7,8},{8,7},{9,10},{10,9},{11,... | collective-permute-start | bytes 98312 | tf_op jit(solution)/shard_map/ppermute | solution.py:406
  15.8 0.7 %collective-permute-start.1 = (f32[4,16,128]{2,1,0:T(8,128)S(1)}, f32[4,16,128]{2,1,0:T(8,128)S(1)}, u32[]{:S(2)}, u32[]{:S(2)}) collective-permute-start(f32[4,16,128]{2,1,0:T(8,128)S(1)} %get-tuple-element.7), channel_id=1, source_target_pairs={{32,64},{64,32},{33,65},{65,33},{34,66},{66,34},{35,67},{67,35},{3... | collective-permute-start | bytes 98312 | tf_op jit(solution)/shard_map/ppermute | solution.py:406
  16.4 4.6 %collective-permute-start.2 = (f32[4,4,512]{2,1,0:T(4,128)S(1)}, f32[4,4,512]{2,1,0:T(4,128)S(1)}, u32[]{:S(2)}, u32[]{:S(2)}) collective-permute-start(f32[4,4,512]{2,1,0:T(4,128)S(1)} %get-tuple-element.8), channel_id=1, source_target_pairs={{0,1},{1,0},{2,3},{3,2},{4,5},{5,4},{6,7},{7,6},{8,9},{9,8},{10,11... | collective-permute-start | bytes 98312 | tf_op jit(solution)/shard_map/ppermute | solution.py:406
  21.0 1.7 %collective-permute-start.3 = (f32[4,16,128]{2,1,0:T(8,128)S(1)}, f32[4,16,128]{2,1,0:T(8,128)S(1)}, u32[]{:S(2)}, u32[]{:S(2)}) collective-permute-start(f32[4,16,128]{2,1,0:T(8,128)S(1)} %get-tuple-element.9), channel_id=1, source_target_pairs={{0,32},{32,0},{64,96},{96,64},{1,33},{33,1},{65,97},{97,65},{2,34}... | collective-permute-start | bytes 98312 | tf_op jit(solution)/shard_map/ppermute | solution.py:406
  22.7 0.0 copy-done.1
  22.7 0.0 copy-done.2
  22.7 0.0 copy-done.3
  22.7 2.2 %shard_map.86.new_ref = f32[4,8,16,512]{3,2,1,0:T(8,128)S(1)} custom-call(s32[1,128]{1,0:T(1,128)S(1)} %bitcast.2, f32[1,128]{1,0:T(1,128)S(1)} %bitcast.3, f32[4,8,4,4,512]{4,3,2,1,0:T(4,128)S(1)} %copy-done, f32[64,128]{1,0:T(8,128)S(1)} %copy-done.3), custom_call_target="tpu_custom_call" | custom-call | flops 4000000000 | bytes 4000000 | tf_op jit(solution)/shard_map/pallas_call | solution.py:438
  24.9 0.0 copy-done.4
  24.9 0.1 copy.9.arrival_ref
  25.0 0.0 collective-permute-done.cross_two
  25.0 0.0 collective-permute-done.1.along_two
  25.0 0.0 collective-permute-done.2.cross_one
  25.0 0.0 collective-permute-done.3.along_one
  25.0 2.8 %all-to-all-done.received_ref = f32[32,8,512]{2,1,0:T(8,128)S(1)} async-done(((f32[32,8,512]{2,1,0:T(8,128)}), f32[32,8,512]{2,1,0:T(8,128)S(1)}, u32[]{:S(2)}, u32[]{:S(2)}) %all-to-all-start) | async-done | bytes 524320 | tf_op jit(solution)/shard_map/all_to_all | solution.py:430
  27.9 1.9 %shard_map.89 = (f32[4,8,4,4,512]{4,3,2,1,0:T(4,128)}, f32[8,4,4,512]{3,2,1,0:T(4,128)}) custom-call(s32[8,4]{1,0:T(8,128)S(1)} %copy.9.arrival_ref, f32[4,8,4,4,512]{4,3,2,1,0:T(4,128)S(1)} %copy-done, f32[4,8,16,512]{3,2,1,0:T(8,128)S(1)} %shard_map.86.new_ref, f32[4,4,512]{2,1,0:T(4,128)S(1)} %collective-permute-done.cross_two, ...), custom_call_target="tpu_custom_call" | custom-call | flops 10000000 | bytes 4000000 | tf_op jit(solution)/shard_map/pallas_call | solution.py:458
  (1 shorter events, 0.0 us)
Async XLA Ops:
  3.7 11.1 %copy-start = (f32[4,8,4,4,512]{4,3,2,1,0:T(4,128)S(1)}, f32[4,8,4,4,512]{4,3,2,1,0:T(4,128)}, u32[]{:S(2)}) copy-start(f32[4,8,4,4,512]{4,3,2,1,0:T(4,128)} %adj_ref.5) | copy-start | bytes 3145732
  3.7 19.0 %copy-start.1 = (s32[128]{0:T(128)S(1)}, s32[128]{0:T(128)}, u32[]{:S(2)}) copy-start(s32[128]{0:T(128)} %param.11) | copy-start | bytes 1540
  3.7 19.0 %copy-start.2 = (f32[128]{0:T(128)S(1)}, f32[128]{0:T(128)}, u32[]{:S(2)}) copy-start(f32[128]{0:T(128)} %param.12) | copy-start | bytes 1540
  3.7 19.0 %copy-start.3 = (f32[64,128]{1,0:T(8,128)S(1)}, f32[64,128]{1,0:T(8,128)}, u32[]{:S(2)}) copy-start(f32[64,128]{1,0:T(8,128)} %constant.2.clone.rows_ref.rows_hbm) | copy-start | bytes 98308
  3.7 24.2 %all-to-all-start = ((f32[32,8,512]{2,1,0:T(8,128)}), f32[32,8,512]{2,1,0:T(8,128)S(1)}, u32[]{:S(2)}, u32[]{:S(2)}) async-start(f32[32,8,512]{2,1,0:T(8,128)} %shard_map.88), calls=%async_computation | async-start | bytes 1048576 | tf_op jit(solution)/shard_map/all_to_all | solution.py:430
  15.1 9.9 %collective-permute-start = (f32[4,4,512]{2,1,0:T(4,128)S(1)}, f32[4,4,512]{2,1,0:T(4,128)S(1)}, u32[]{:S(2)}, u32[]{:S(2)}) collective-permute-start(f32[4,4,512]{2,1,0:T(4,128)S(1)} %get-tuple-element.6), channel_id=1, source_target_pairs={{1,2},{2,1},{3,4},{4,3},{5,6},{6,5},{7,8},{8,7},{9,10},{10,9},{11,... | collective-permute-start | bytes 98312 | tf_op jit(solution)/shard_map/ppermute | solution.py:406
  15.8 9.3 %collective-permute-start.1 = (f32[4,16,128]{2,1,0:T(8,128)S(1)}, f32[4,16,128]{2,1,0:T(8,128)S(1)}, u32[]{:S(2)}, u32[]{:S(2)}) collective-permute-start(f32[4,16,128]{2,1,0:T(8,128)S(1)} %get-tuple-element.7), channel_id=1, source_target_pairs={{32,64},{64,32},{33,65},{65,33},{34,66},{66,34},{35,67},{67,35},{3... | collective-permute-start | bytes 98312 | tf_op jit(solution)/shard_map/ppermute | solution.py:406
  16.4 8.6 %collective-permute-start.2 = (f32[4,4,512]{2,1,0:T(4,128)S(1)}, f32[4,4,512]{2,1,0:T(4,128)S(1)}, u32[]{:S(2)}, u32[]{:S(2)}) collective-permute-start(f32[4,4,512]{2,1,0:T(4,128)S(1)} %get-tuple-element.8), channel_id=1, source_target_pairs={{0,1},{1,0},{2,3},{3,2},{4,5},{5,4},{6,7},{7,6},{8,9},{9,8},{10,11... | collective-permute-start | bytes 98312 | tf_op jit(solution)/shard_map/ppermute | solution.py:406
  21.0 4.0 %collective-permute-start.3 = (f32[4,16,128]{2,1,0:T(8,128)S(1)}, f32[4,16,128]{2,1,0:T(8,128)S(1)}, u32[]{:S(2)}, u32[]{:S(2)}) collective-permute-start(f32[4,16,128]{2,1,0:T(8,128)S(1)} %get-tuple-element.9), channel_id=1, source_target_pairs={{0,32},{32,0},{64,96},{96,64},{1,33},{33,1},{65,97},{97,65},{2,34}... | collective-permute-start | bytes 98312 | tf_op jit(solution)/shard_map/ppermute | solution.py:406
  22.7 2.2 %copy-start.4 = (s32[8,4]{0,1:T(4,128)S(1)}, s32[8,4]{0,1:T(4,128)}, u32[]{:S(2)}) copy-start(s32[8,4]{0,1:T(4,128)} %param.10) | copy-start | bytes 388

commit v6 on v5

--- a/solution.py
+++ b/solution.py
@@ -23,6 +23,7 @@
 F32 = jnp.float32
 BF16 = jnp.bfloat16
 VMEM_BYTES = 24 * 1024 * 1024
+PEER_ORDER = (31, 23, 18, 4, 12, 21, 8, 19, 28, 3, 2, 1, 24, 26, 14, 11, 17, 0, 7, 27, 29, 5, 16, 25, 6, 15, 9, 20, 30, 22, 13, 10)
 HOLDER_BYTES = 60_000_000
 
 
@@ -134,20 +135,17 @@
     copies[0].wait()
     copies[1].wait()
 
-    def gather(g, carry):
-        rows = pl.ds(pl.multiple_of(g * 16, 16), 16)
+    for g in range(16):
+        rows = slice(16 * g, 16 * g + 16)
         for m in range(4):
-            slot = slot_ref[4 * g + m]
+            slot = slot_ref[2 * PEER_ORDER[2 * g + m // 2] + m % 2]
             for f in range(3):
                 stage[f, g, 4 * m : 4 * m + 4, :] = store_ref[slot, f]
         slopes = along_slope([stage[0, g, :, tile(t)] for t in range(4)], rows_ref)
         for t in range(4):
-            total[pl.ds(2 * g, 2), :, tile(t)] = slopes[t].reshape(2, 8, 128)
+            total[slice(2 * g, 2 * g + 2), :, tile(t)] = slopes[t].reshape(2, 8, 128)
         for f in range(2):
             high[f, rows], low[f, rows] = split(stage[f + 1, g])
-        return carry
-
-    lax.fori_loop(0, 16, gather, 0, unroll=16)
     writes = []
     for c in range(2):
         part = slice(256 * c, 256 * c + 256)
@@ -308,8 +306,10 @@
 
 def finish_kernel(
     arrival_ref, adj_ref, new_ref, cross_two, along_two, cross_one, along_one, received_ref,
-    next_hbm, kappa_hbm, next_ref, kappa_ref, edge, side, sems,
+    next_hbm, kappa_hbm, next_ref, kappa_ref, edge, side, place, sems,
 ):
+    for n, peer in enumerate(PEER_ORDER):
+        place[peer] = n
     lift = TIME_STEP * HALF_LIFT
     lane = lanes((4, 128))
     j = (lane >> 3) & 7
@@ -367,7 +367,7 @@
         for c in range(4):
             q = arrival_ref[a, c]
             clipped = jnp.maximum(q, 0)
-            holder = clipped >> 1
+            holder = place[clipped >> 1]
             second = (clipped & 1) == 1
             block = jnp.where(second, received_ref[holder, 4:8, :], received_ref[holder, 0:4, :])
             value = TIME_STEP * adj_ref[0, a, c] * block
@@ -427,7 +427,9 @@
         HBM,
         HOLDER_BYTES,
     )(dispatch_slot, snapshot_store, rows)
-    received = lax.all_to_all(outgoing, "cross", split_axis=0, concat_axis=0, tiled=True)
+    received = lax.all_to_all(
+        outgoing, "cross", split_axis=0, concat_axis=0, axis_index_groups=[list(PEER_ORDER)], tiled=True
+    )
     along_one, along_two, cross_one, cross_two = kernel(
         trace_kernel,
         (array(4, 16, 128), array(4, 16, 128), array(4, 4, 512), array(4, 4, 512)),
@@ -464,6 +466,7 @@
             pltpu.VMEM((8, 4, 4, 512), F32),
             pltpu.VMEM((2, 4, 16, 128), F32),
             pltpu.VMEM((2, 4, 4, 512), F32),
+            pltpu.SMEM((32,), jnp.int32),
             pltpu.SemaphoreType.DMA((5,)),
         ],
         10_000_000, 4_000_000,

time: 30 us -> 28.2 us (0.940)
  the two profiles are of different devices: /device:TPU:0 before, /device:TPU:32 now
where the time goes in v6:
time: 28.2 us; the launch traced here: 27.9 us
  starting transfers between devices  17.5 us (62%)
  Pallas kernels  7.48 us (27%)
  waiting for transfers between devices  2.03 us (7%)
  between operations  0.74 us (3%)
    all_to_all x1, starting transfers between devices, per_device(): lax.all_to_all(outgoing, 'cross', split_axis=0, concat_axis=0, axis_index...  11.6 us
    ppermute x4, starting transfers between devices, exchange(): return lax.ppermute(value, axis, pairs)  5.94 us
    pallas_call x1, Pallas kernels, per_device(): kernel(holder_kernel, array(32, 8, 512), [HBM] * 3, [pltpu.SMEM((64,), jn...  3.06 us
    pallas_call x1, Pallas kernels, per_device(): kernel(volume_kernel, array(4, 8, 16, 512), [VMEM] * 4, [pltpu.VMEM((2, 5...  2.23 us
    ppermute x4, waiting for transfers between devices, exchange(): return lax.ppermute(value, axis, pairs)  2.03 us
    pallas_call x1, Pallas kernels, per_device(): kernel(finish_kernel, (array(4, 8, 4, 4, 512), array(8, 4, 4, 512)), [SME...  1.88 us
  transfers between devices with their start and end apart: 5, of which 1 were waited for; matrix products, arithmetic and copies ran while one was open for 0% of the time, Pallas kernels for 9%

profile of v6, /device:TPU:32, one launch (start us, length us, event | category | flops | bytes accessed | tf_op | source)
XLA Modules:
  0.0 27.9 jit_solution(17963865220506506825)
XLA Ops:
  0.6 3.1 %shard_map.88 = f32[32,8,512]{2,1,0:T(8,128)} custom-call(s32[64]{0:T(128)} %slot_hbm.1, f32[64,3,4,512]{3,2,1,0:T(4,128)} %store_hbm.1, f32[64,128]{1,0:T(8,128)} %constant.2.clone.rows_ref.rows_hbm), custom_call_target="tpu_custom_call" | custom-call | flops 3000000000 | bytes 5000000 | tf_op jit(solution)/shard_map/pallas_call | solution.py:411
  3.7 0.0 copy-start
  3.7 0.0 copy-start.1
  3.7 0.0 copy-start.2
  3.7 0.0 copy-start.3
  3.7 11.6 %all-to-all-start = ((f32[32,8,512]{2,1,0:T(8,128)}), f32[32,8,512]{2,1,0:T(8,128)S(1)}, u32[]{:S(2)}, u32[]{:S(2)}) async-start(f32[32,8,512]{2,1,0:T(8,128)} %shard_map.88), calls=%async_computation | async-start | bytes 1048576 | tf_op jit(solution)/shard_map/all_to_all | solution.py:430
  15.4 0.0 copy-done
  15.4 0.3 %shard_map.87 = (f32[4,16,128]{2,1,0:T(8,128)S(1)}, f32[4,16,128]{2,1,0:T(8,128)S(1)}, f32[4,4,512]{2,1,0:T(4,128)S(1)}, f32[4,4,512]{2,1,0:T(4,128)S(1)}) custom-call(f32[4,8,4,4,512]{4,3,2,1,0:T(4,128)S(1)} %copy-done), custom_call_target="tpu_custom_call" | custom-call | flops 1000000 | bytes 500000 | tf_op jit(solution)/shard_map/pallas_call | solution.py:433
  15.7 3.2 %collective-permute-start = (f32[4,4,512]{2,1,0:T(4,128)S(1)}, f32[4,4,512]{2,1,0:T(4,128)S(1)}, u32[]{:S(2)}, u32[]{:S(2)}) collective-permute-start(f32[4,4,512]{2,1,0:T(4,128)S(1)} %get-tuple-element.6), channel_id=1, source_target_pairs={{1,2},{2,1},{3,4},{4,3},{5,6},{6,5},{7,8},{8,7},{9,10},{10,9},{11,... | collective-permute-start | bytes 98312 | tf_op jit(solution)/shard_map/ppermute | solution.py:406
  18.8 0.7 %collective-permute-start.1 = (f32[4,16,128]{2,1,0:T(8,128)S(1)}, f32[4,16,128]{2,1,0:T(8,128)S(1)}, u32[]{:S(2)}, u32[]{:S(2)}) collective-permute-start(f32[4,16,128]{2,1,0:T(8,128)S(1)} %get-tuple-element.7), channel_id=1, source_target_pairs={{32,64},{64,32},{33,65},{65,33},{34,66},{66,34},{35,67},{67,35},{3... | collective-permute-start | bytes 98312 | tf_op jit(solution)/shard_map/ppermute | solution.py:406
  19.5 0.4 %collective-permute-start.2 = (f32[4,4,512]{2,1,0:T(4,128)S(1)}, f32[4,4,512]{2,1,0:T(4,128)S(1)}, u32[]{:S(2)}, u32[]{:S(2)}) collective-permute-start(f32[4,4,512]{2,1,0:T(4,128)S(1)} %get-tuple-element.8), channel_id=1, source_target_pairs={{0,1},{1,0},{2,3},{3,2},{4,5},{5,4},{6,7},{7,6},{8,9},{9,8},{10,11... | collective-permute-start | bytes 98312 | tf_op jit(solution)/shard_map/ppermute | solution.py:406
  19.9 1.7 %collective-permute-start.3 = (f32[4,16,128]{2,1,0:T(8,128)S(1)}, f32[4,16,128]{2,1,0:T(8,128)S(1)}, u32[]{:S(2)}, u32[]{:S(2)}) collective-permute-start(f32[4,16,128]{2,1,0:T(8,128)S(1)} %get-tuple-element.9), channel_id=1, source_target_pairs={{0,32},{32,0},{64,96},{96,64},{1,33},{33,1},{65,97},{97,65},{2,34}... | collective-permute-start | bytes 98312 | tf_op jit(solution)/shard_map/ppermute | solution.py:406
  21.6 0.0 copy-done.1
  21.6 0.0 copy-done.2
  21.6 0.0 copy-done.3
  21.7 2.2 %shard_map.86.new_ref = f32[4,8,16,512]{3,2,1,0:T(8,128)S(1)} custom-call(s32[1,128]{1,0:T(1,128)S(1)} %bitcast.2, f32[1,128]{1,0:T(1,128)S(1)} %bitcast.3, f32[4,8,4,4,512]{4,3,2,1,0:T(4,128)S(1)} %copy-done, f32[64,128]{1,0:T(8,128)S(1)} %copy-done.3), custom_call_target="tpu_custom_call" | custom-call | flops 4000000000 | bytes 4000000 | tf_op jit(solution)/shard_map/pallas_call | solution.py:440
  23.9 0.0 copy-done.4
  23.9 0.1 copy.9.arrival_ref
  24.0 2.0 %collective-permute-done.cross_two = f32[4,4,512]{2,1,0:T(4,128)S(1)} collective-permute-done((f32[4,4,512]{2,1,0:T(4,128)S(1)}, f32[4,4,512]{2,1,0:T(4,128)S(1)}, u32[]{:S(2)}, u32[]{:S(2)}) %collective-permute-start) | collective-permute-done | bytes 32800 | tf_op jit(solution)/shard_map/ppermute | solution.py:406
  26.0 0.0 collective-permute-done.1.along_two
  26.0 0.0 collective-permute-done.2.cross_one
  26.0 0.0 collective-permute-done.3.along_one
  26.0 0.0 all-to-all-done.received_ref
  26.0 1.9 %shard_map.89 = (f32[4,8,4,4,512]{4,3,2,1,0:T(4,128)}, f32[8,4,4,512]{3,2,1,0:T(4,128)}) custom-call(s32[8,4]{1,0:T(8,128)S(1)} %copy.9.arrival_ref, f32[4,8,4,4,512]{4,3,2,1,0:T(4,128)S(1)} %copy-done, f32[4,8,16,512]{3,2,1,0:T(8,128)S(1)} %shard_map.86.new_ref, f32[4,4,512]{2,1,0:T(4,128)S(1)} %collective-permute-done.cross_two, ...), custom_call_target="tpu_custom_call" | custom-call | flops 10000000 | bytes 4000000 | tf_op jit(solution)/shard_map/pallas_call | solution.py:460
  (1 shorter events, 0.0 us)
Async XLA Ops:
  3.7 11.7 %copy-start = (f32[4,8,4,4,512]{4,3,2,1,0:T(4,128)S(1)}, f32[4,8,4,4,512]{4,3,2,1,0:T(4,128)}, u32[]{:S(2)}) copy-start(f32[4,8,4,4,512]{4,3,2,1,0:T(4,128)} %adj_ref.5) | copy-start | bytes 3145732
  3.7 17.9 %copy-start.1 = (s32[128]{0:T(128)S(1)}, s32[128]{0:T(128)}, u32[]{:S(2)}) copy-start(s32[128]{0:T(128)} %param.11) | copy-start | bytes 1540
  3.7 17.9 %copy-start.2 = (f32[128]{0:T(128)S(1)}, f32[128]{0:T(128)}, u32[]{:S(2)}) copy-start(f32[128]{0:T(128)} %param.12) | copy-start | bytes 1540
  3.7 17.9 %copy-start.3 = (f32[64,128]{1,0:T(8,128)S(1)}, f32[64,128]{1,0:T(8,128)}, u32[]{:S(2)}) copy-start(f32[64,128]{1,0:T(8,128)} %constant.2.clone.rows_ref.rows_hbm) | copy-start | bytes 98308
  3.7 22.3 %all-to-all-start = ((f32[32,8,512]{2,1,0:T(8,128)}), f32[32,8,512]{2,1,0:T(8,128)S(1)}, u32[]{:S(2)}, u32[]{:S(2)}) async-start(f32[32,8,512]{2,1,0:T(8,128)} %shard_map.88), calls=%async_computation | async-start | bytes 1048576 | tf_op jit(solution)/shard_map/all_to_all | solution.py:430
  15.7 10.3 %collective-permute-start = (f32[4,4,512]{2,1,0:T(4,128)S(1)}, f32[4,4,512]{2,1,0:T(4,128)S(1)}, u32[]{:S(2)}, u32[]{:S(2)}) collective-permute-start(f32[4,4,512]{2,1,0:T(4,128)S(1)} %get-tuple-element.6), channel_id=1, source_target_pairs={{1,2},{2,1},{3,4},{4,3},{5,6},{6,5},{7,8},{8,7},{9,10},{10,9},{11,... | collective-permute-start | bytes 98312 | tf_op jit(solution)/shard_map/ppermute | solution.py:406
  18.8 7.2 %collective-permute-start.1 = (f32[4,16,128]{2,1,0:T(8,128)S(1)}, f32[4,16,128]{2,1,0:T(8,128)S(1)}, u32[]{:S(2)}, u32[]{:S(2)}) collective-permute-start(f32[4,16,128]{2,1,0:T(8,128)S(1)} %get-tuple-element.7), channel_id=1, source_target_pairs={{32,64},{64,32},{33,65},{65,33},{34,66},{66,34},{35,67},{67,35},{3... | collective-permute-start | bytes 98312 | tf_op jit(solution)/shard_map/ppermute | solution.py:406
  19.5 6.5 %collective-permute-start.2 = (f32[4,4,512]{2,1,0:T(4,128)S(1)}, f32[4,4,512]{2,1,0:T(4,128)S(1)}, u32[]{:S(2)}, u32[]{:S(2)}) collective-permute-start(f32[4,4,512]{2,1,0:T(4,128)S(1)} %get-tuple-element.8), channel_id=1, source_target_pairs={{0,1},{1,0},{2,3},{3,2},{4,5},{5,4},{6,7},{7,6},{8,9},{9,8},{10,11... | collective-permute-start | bytes 98312 | tf_op jit(solution)/shard_map/ppermute | solution.py:406
  19.9 6.1 %collective-permute-start.3 = (f32[4,16,128]{2,1,0:T(8,128)S(1)}, f32[4,16,128]{2,1,0:T(8,128)S(1)}, u32[]{:S(2)}, u32[]{:S(2)}) collective-permute-start(f32[4,16,128]{2,1,0:T(8,128)S(1)} %get-tuple-element.9), channel_id=1, source_target_pairs={{0,32},{32,0},{64,96},{96,64},{1,33},{33,1},{65,97},{97,65},{2,34}... | collective-permute-start | bytes 98312 | tf_op jit(solution)/shard_map/ppermute | solution.py:406
  21.6 2.2 %copy-start.4 = (s32[8,4]{0,1:T(4,128)S(1)}, s32[8,4]{0,1:T(4,128)}, u32[]{:S(2)}) copy-start(s32[8,4]{0,1:T(4,128)} %param.10) | copy-start | bytes 388

commit v7 on v6

--- a/solution.py
+++ b/solution.py
@@ -23,7 +23,7 @@
 F32 = jnp.float32
 BF16 = jnp.bfloat16
 VMEM_BYTES = 24 * 1024 * 1024
-PEER_ORDER = (31, 23, 18, 4, 12, 21, 8, 19, 28, 3, 2, 1, 24, 26, 14, 11, 17, 0, 7, 27, 29, 5, 16, 25, 6, 15, 9, 20, 30, 22, 13, 10)
+PEER_ORDER = (31, 23, 28, 26, 12, 21, 8, 19, 18, 3, 2, 1, 24, 4, 14, 11, 17, 0, 7, 27, 22, 5, 16, 25, 6, 15, 9, 10, 30, 29, 13, 20)
 HOLDER_BYTES = 60_000_000
 
 

time: 28.2 us -> 28.2 us (level)
  no operation moved by 1% of the time
where the time goes in v7:
time: 28.2 us; the launch traced here: 27.9 us
  starting transfers between devices  17.6 us (62%)
  Pallas kernels  7.47 us (26%)
  waiting for transfers between devices  2.02 us (7%)
  between operations  0.74 us (3%)
    all_to_all x1, starting transfers between devices, per_device(): lax.all_to_all(outgoing, 'cross', split_axis=0, concat_axis=0, axis_index...  11.6 us
    ppermute x4, starting transfers between devices, exchange(): return lax.ppermute(value, axis, pairs)  5.95 us
    pallas_call x1, Pallas kernels, per_device(): kernel(holder_kernel, array(32, 8, 512), [HBM] * 3, [pltpu.SMEM((64,), jn...  3.06 us
    pallas_call x1, Pallas kernels, per_device(): kernel(volume_kernel, array(4, 8, 16, 512), [VMEM] * 4, [pltpu.VMEM((2, 5...  2.23 us
    ppermute x4, waiting for transfers between devices, exchange(): return lax.ppermute(value, axis, pairs)  2.02 us
    pallas_call x1, Pallas kernels, per_device(): kernel(finish_kernel, (array(4, 8, 4, 4, 512), array(8, 4, 4, 512)), [SME...  1.88 us
  transfers between devices with their start and end apart: 5, of which 1 were waited for; matrix products, arithmetic and copies ran while one was open for 0% of the time, Pallas kernels for 9%

profile of v7, /device:TPU:32, one launch (start us, length us, event | category | flops | bytes accessed | tf_op | source)
XLA Modules:
  0.0 27.9 jit_solution(10042191778029199362)
XLA Ops:
  0.6 3.1 %shard_map.88 = f32[32,8,512]{2,1,0:T(8,128)} custom-call(s32[64]{0:T(128)} %slot_hbm.1, f32[64,3,4,512]{3,2,1,0:T(4,128)} %store_hbm.1, f32[64,128]{1,0:T(8,128)} %constant.2.clone.rows_ref.rows_hbm), custom_call_target="tpu_custom_call" | custom-call | flops 3000000000 | bytes 5000000 | tf_op jit(solution)/shard_map/pallas_call | solution.py:411
  3.7 0.0 copy-start
  3.7 0.0 copy-start.1
  3.7 0.0 copy-start.2
  3.7 0.0 copy-start.3
  3.7 11.6 %all-to-all-start = ((f32[32,8,512]{2,1,0:T(8,128)}), f32[32,8,512]{2,1,0:T(8,128)S(1)}, u32[]{:S(2)}, u32[]{:S(2)}) async-start(f32[32,8,512]{2,1,0:T(8,128)} %shard_map.88), calls=%async_computation | async-start | bytes 1048576 | tf_op jit(solution)/shard_map/all_to_all | solution.py:430
  15.4 0.0 copy-done
  15.4 0.3 %shard_map.87 = (f32[4,16,128]{2,1,0:T(8,128)S(1)}, f32[4,16,128]{2,1,0:T(8,128)S(1)}, f32[4,4,512]{2,1,0:T(4,128)S(1)}, f32[4,4,512]{2,1,0:T(4,128)S(1)}) custom-call(f32[4,8,4,4,512]{4,3,2,1,0:T(4,128)S(1)} %copy-done), custom_call_target="tpu_custom_call" | custom-call | flops 1000000 | bytes 500000 | tf_op jit(solution)/shard_map/pallas_call | solution.py:433
  15.7 3.2 %collective-permute-start = (f32[4,4,512]{2,1,0:T(4,128)S(1)}, f32[4,4,512]{2,1,0:T(4,128)S(1)}, u32[]{:S(2)}, u32[]{:S(2)}) collective-permute-start(f32[4,4,512]{2,1,0:T(4,128)S(1)} %get-tuple-element.6), channel_id=1, source_target_pairs={{1,2},{2,1},{3,4},{4,3},{5,6},{6,5},{7,8},{8,7},{9,10},{10,9},{11,... | collective-permute-start | bytes 98312 | tf_op jit(solution)/shard_map/ppermute | solution.py:406
  18.8 0.7 %collective-permute-start.1 = (f32[4,16,128]{2,1,0:T(8,128)S(1)}, f32[4,16,128]{2,1,0:T(8,128)S(1)}, u32[]{:S(2)}, u32[]{:S(2)}) collective-permute-start(f32[4,16,128]{2,1,0:T(8,128)S(1)} %get-tuple-element.7), channel_id=1, source_target_pairs={{32,64},{64,32},{33,65},{65,33},{34,66},{66,34},{35,67},{67,35},{3... | collective-permute-start | bytes 98312 | tf_op jit(solution)/shard_map/ppermute | solution.py:406
  19.5 0.4 %collective-permute-start.2 = (f32[4,4,512]{2,1,0:T(4,128)S(1)}, f32[4,4,512]{2,1,0:T(4,128)S(1)}, u32[]{:S(2)}, u32[]{:S(2)}) collective-permute-start(f32[4,4,512]{2,1,0:T(4,128)S(1)} %get-tuple-element.8), channel_id=1, source_target_pairs={{0,1},{1,0},{2,3},{3,2},{4,5},{5,4},{6,7},{7,6},{8,9},{9,8},{10,11... | collective-permute-start | bytes 98312 | tf_op jit(solution)/shard_map/ppermute | solution.py:406
  19.9 1.7 %collective-permute-start.3 = (f32[4,16,128]{2,1,0:T(8,128)S(1)}, f32[4,16,128]{2,1,0:T(8,128)S(1)}, u32[]{:S(2)}, u32[]{:S(2)}) collective-permute-start(f32[4,16,128]{2,1,0:T(8,128)S(1)} %get-tuple-element.9), channel_id=1, source_target_pairs={{0,32},{32,0},{64,96},{96,64},{1,33},{33,1},{65,97},{97,65},{2,34}... | collective-permute-start | bytes 98312 | tf_op jit(solution)/shard_map/ppermute | solution.py:406
  21.6 0.0 copy-done.1
  21.6 0.0 copy-done.2
  21.6 0.0 copy-done.3
  21.7 2.2 %shard_map.86.new_ref = f32[4,8,16,512]{3,2,1,0:T(8,128)S(1)} custom-call(s32[1,128]{1,0:T(1,128)S(1)} %bitcast.2, f32[1,128]{1,0:T(1,128)S(1)} %bitcast.3, f32[4,8,4,4,512]{4,3,2,1,0:T(4,128)S(1)} %copy-done, f32[64,128]{1,0:T(8,128)S(1)} %copy-done.3), custom_call_target="tpu_custom_call" | custom-call | flops 4000000000 | bytes 4000000 | tf_op jit(solution)/shard_map/pallas_call | solution.py:440
  23.9 0.0 copy-done.4
  23.9 0.1 copy.9.arrival_ref
  24.0 2.0 %collective-permute-done.cross_two = f32[4,4,512]{2,1,0:T(4,128)S(1)} collective-permute-done((f32[4,4,512]{2,1,0:T(4,128)S(1)}, f32[4,4,512]{2,1,0:T(4,128)S(1)}, u32[]{:S(2)}, u32[]{:S(2)}) %collective-permute-start) | collective-permute-done | bytes 32800 | tf_op jit(solution)/shard_map/ppermute | solution.py:406
  26.0 0.0 collective-permute-done.1.along_two
  26.0 0.0 collective-permute-done.2.cross_one
  26.0 0.0 collective-permute-done.3.along_one
  26.0 0.0 all-to-all-done.received_ref
  26.0 1.9 %shard_map.89 = (f32[4,8,4,4,512]{4,3,2,1,0:T(4,128)}, f32[8,4,4,512]{3,2,1,0:T(4,128)}) custom-call(s32[8,4]{1,0:T(8,128)S(1)} %copy.9.arrival_ref, f32[4,8,4,4,512]{4,3,2,1,0:T(4,128)S(1)} %copy-done, f32[4,8,16,512]{3,2,1,0:T(8,128)S(1)} %shard_map.86.new_ref, f32[4,4,512]{2,1,0:T(4,128)S(1)} %collective-permute-done.cross_two, ...), custom_call_target="tpu_custom_call" | custom-call | flops 10000000 | bytes 4000000 | tf_op jit(solution)/shard_map/pallas_call | solution.py:460
  (1 shorter events, 0.0 us)
Async XLA Ops:
  3.7 11.7 %copy-start = (f32[4,8,4,4,512]{4,3,2,1,0:T(4,128)S(1)}, f32[4,8,4,4,512]{4,3,2,1,0:T(4,128)}, u32[]{:S(2)}) copy-start(f32[4,8,4,4,512]{4,3,2,1,0:T(4,128)} %adj_ref.5) | copy-start | bytes 3145732
  3.7 17.9 %copy-start.1 = (s32[128]{0:T(128)S(1)}, s32[128]{0:T(128)}, u32[]{:S(2)}) copy-start(s32[128]{0:T(128)} %param.11) | copy-start | bytes 1540
  3.7 17.9 %copy-start.2 = (f32[128]{0:T(128)S(1)}, f32[128]{0:T(128)}, u32[]{:S(2)}) copy-start(f32[128]{0:T(128)} %param.12) | copy-start | bytes 1540
  3.7 17.9 %copy-start.3 = (f32[64,128]{1,0:T(8,128)S(1)}, f32[64,128]{1,0:T(8,128)}, u32[]{:S(2)}) copy-start(f32[64,128]{1,0:T(8,128)} %constant.2.clone.rows_ref.rows_hbm) | copy-start | bytes 98308
  3.7 22.3 %all-to-all-start = ((f32[32,8,512]{2,1,0:T(8,128)}), f32[32,8,512]{2,1,0:T(8,128)S(1)}, u32[]{:S(2)}, u32[]{:S(2)}) async-start(f32[32,8,512]{2,1,0:T(8,128)} %shard_map.88), calls=%async_computation | async-start | bytes 1048576 | tf_op jit(solution)/shard_map/all_to_all | solution.py:430
  15.7 10.3 %collective-permute-start = (f32[4,4,512]{2,1,0:T(4,128)S(1)}, f32[4,4,512]{2,1,0:T(4,128)S(1)}, u32[]{:S(2)}, u32[]{:S(2)}) collective-permute-start(f32[4,4,512]{2,1,0:T(4,128)S(1)} %get-tuple-element.6), channel_id=1, source_target_pairs={{1,2},{2,1},{3,4},{4,3},{5,6},{6,5},{7,8},{8,7},{9,10},{10,9},{11,... | collective-permute-start | bytes 98312 | tf_op jit(solution)/shard_map/ppermute | solution.py:406
  18.8 7.2 %collective-permute-start.1 = (f32[4,16,128]{2,1,0:T(8,128)S(1)}, f32[4,16,128]{2,1,0:T(8,128)S(1)}, u32[]{:S(2)}, u32[]{:S(2)}) collective-permute-start(f32[4,16,128]{2,1,0:T(8,128)S(1)} %get-tuple-element.7), channel_id=1, source_target_pairs={{32,64},{64,32},{33,65},{65,33},{34,66},{66,34},{35,67},{67,35},{3... | collective-permute-start | bytes 98312 | tf_op jit(solution)/shard_map/ppermute | solution.py:406
  19.5 6.5 %collective-permute-start.2 = (f32[4,4,512]{2,1,0:T(4,128)S(1)}, f32[4,4,512]{2,1,0:T(4,128)S(1)}, u32[]{:S(2)}, u32[]{:S(2)}) collective-permute-start(f32[4,4,512]{2,1,0:T(4,128)S(1)} %get-tuple-element.8), channel_id=1, source_target_pairs={{0,1},{1,0},{2,3},{3,2},{4,5},{5,4},{6,7},{7,6},{8,9},{9,8},{10,11... | collective-permute-start | bytes 98312 | tf_op jit(solution)/shard_map/ppermute | solution.py:406
  19.9 6.1 %collective-permute-start.3 = (f32[4,16,128]{2,1,0:T(8,128)S(1)}, f32[4,16,128]{2,1,0:T(8,128)S(1)}, u32[]{:S(2)}, u32[]{:S(2)}) collective-permute-start(f32[4,16,128]{2,1,0:T(8,128)S(1)} %get-tuple-element.9), channel_id=1, source_target_pairs={{0,32},{32,0},{64,96},{96,64},{1,33},{33,1},{65,97},{97,65},{2,34}... | collective-permute-start | bytes 98312 | tf_op jit(solution)/shard_map/ppermute | solution.py:406
  21.6 2.2 %copy-start.4 = (s32[8,4]{0,1:T(4,128)S(1)}, s32[8,4]{0,1:T(4,128)}, u32[]{:S(2)}) copy-start(s32[8,4]{0,1:T(4,128)} %param.10) | copy-start | bytes 388

commit v8 on v7

--- a/solution.py
+++ b/solution.py
@@ -361,8 +361,10 @@
                     if t == 3 and a == 7:
                         value = value + edge[1, f, 4 * c : 4 * c + 4, :]
                     next_ref[f, a, c, :, tile(t)] = value
-        writes.append(pltpu.make_async_copy(next_ref.at[f], next_hbm.at[f], sems.at[f]))
-        writes[f].start()
+        if f % 2 == 1:
+            pair = slice(f - 1, f + 1)
+            writes.append(pltpu.make_async_copy(next_ref.at[pair], next_hbm.at[pair], sems.at[f]))
+            writes[-1].start()
     for a in range(8):
         for c in range(4):
             q = arrival_ref[a, c]
@@ -373,7 +375,7 @@
             value = TIME_STEP * adj_ref[0, a, c] * block
             kappa_ref[a, c] = jnp.where(q >= 0, value, 0.0)
     writes.append(pltpu.make_async_copy(kappa_ref, kappa_hbm, sems.at[4]))
-    writes[4].start()
+    writes[-1].start()
     for write in writes:
         write.wait()
 

time: 28.2 us -> 28.3 us (level)
  no operation moved by 1% of the time
where the time goes in v8:
time: 28.3 us; the launch traced here: 28 us
  starting transfers between devices  17.5 us (62%)
  Pallas kernels  7.59 us (27%)
  waiting for transfers between devices  2.03 us (7%)
  between operations  0.74 us (3%)
    all_to_all x1, starting transfers between devices, per_device(): lax.all_to_all(outgoing, 'cross', split_axis=0, concat_axis=0, axis_index...  11.6 us
    ppermute x4, starting transfers between devices, exchange(): return lax.ppermute(value, axis, pairs)  5.94 us
    pallas_call x1, Pallas kernels, per_device(): kernel(holder_kernel, array(32, 8, 512), [HBM] * 3, [pltpu.SMEM((64,), jn...  3.06 us
    pallas_call x1, Pallas kernels, per_device(): kernel(volume_kernel, array(4, 8, 16, 512), [VMEM] * 4, [pltpu.VMEM((2, 5...  2.23 us
    ppermute x4, waiting for transfers between devices, exchange(): return lax.ppermute(value, axis, pairs)  2.03 us
    pallas_call x1, Pallas kernels, per_device(): kernel(finish_kernel, (array(4, 8, 4, 4, 512), array(8, 4, 4, 512)), [SME...  1.99 us
  transfers between devices with their start and end apart: 5, of which 1 were waited for; matrix products, arithmetic and copies ran while one was open for 0% of the time, Pallas kernels for 9%

profile of v8, /device:TPU:32, one launch (start us, length us, event | category | flops | bytes accessed | tf_op | source)
XLA Modules:
  0.0 28.0 jit_solution(8384476076194163951)
XLA Ops:
  0.6 3.1 %shard_map.88 = f32[32,8,512]{2,1,0:T(8,128)} custom-call(s32[64]{0:T(128)} %slot_hbm.1, f32[64,3,4,512]{3,2,1,0:T(4,128)} %store_hbm.1, f32[64,128]{1,0:T(8,128)} %constant.2.clone.rows_ref.rows_hbm), custom_call_target="tpu_custom_call" | custom-call | flops 3000000000 | bytes 5000000 | tf_op jit(solution)/shard_map/pallas_call | solution.py:413
  3.7 0.0 copy-start
  3.7 0.0 copy-start.1
  3.7 0.0 copy-start.2
  3.7 0.0 copy-start.3
  3.7 11.6 %all-to-all-start = ((f32[32,8,512]{2,1,0:T(8,128)}), f32[32,8,512]{2,1,0:T(8,128)S(1)}, u32[]{:S(2)}, u32[]{:S(2)}) async-start(f32[32,8,512]{2,1,0:T(8,128)} %shard_map.88), calls=%async_computation | async-start | bytes 1048576 | tf_op jit(solution)/shard_map/all_to_all | solution.py:432
  15.4 0.0 copy-done
  15.4 0.3 %shard_map.87 = (f32[4,16,128]{2,1,0:T(8,128)S(1)}, f32[4,16,128]{2,1,0:T(8,128)S(1)}, f32[4,4,512]{2,1,0:T(4,128)S(1)}, f32[4,4,512]{2,1,0:T(4,128)S(1)}) custom-call(f32[4,8,4,4,512]{4,3,2,1,0:T(4,128)S(1)} %copy-done), custom_call_target="tpu_custom_call" | custom-call | flops 1000000 | bytes 500000 | tf_op jit(solution)/shard_map/pallas_call | solution.py:435
  15.7 3.2 %collective-permute-start = (f32[4,4,512]{2,1,0:T(4,128)S(1)}, f32[4,4,512]{2,1,0:T(4,128)S(1)}, u32[]{:S(2)}, u32[]{:S(2)}) collective-permute-start(f32[4,4,512]{2,1,0:T(4,128)S(1)} %get-tuple-element.6), channel_id=1, source_target_pairs={{1,2},{2,1},{3,4},{4,3},{5,6},{6,5},{7,8},{8,7},{9,10},{10,9},{11,... | collective-permute-start | bytes 98312 | tf_op jit(solution)/shard_map/ppermute | solution.py:408
  18.8 0.7 %collective-permute-start.1 = (f32[4,16,128]{2,1,0:T(8,128)S(1)}, f32[4,16,128]{2,1,0:T(8,128)S(1)}, u32[]{:S(2)}, u32[]{:S(2)}) collective-permute-start(f32[4,16,128]{2,1,0:T(8,128)S(1)} %get-tuple-element.7), channel_id=1, source_target_pairs={{32,64},{64,32},{33,65},{65,33},{34,66},{66,34},{35,67},{67,35},{3... | collective-permute-start | bytes 98312 | tf_op jit(solution)/shard_map/ppermute | solution.py:408
  19.5 0.4 %collective-permute-start.2 = (f32[4,4,512]{2,1,0:T(4,128)S(1)}, f32[4,4,512]{2,1,0:T(4,128)S(1)}, u32[]{:S(2)}, u32[]{:S(2)}) collective-permute-start(f32[4,4,512]{2,1,0:T(4,128)S(1)} %get-tuple-element.8), channel_id=1, source_target_pairs={{0,1},{1,0},{2,3},{3,2},{4,5},{5,4},{6,7},{7,6},{8,9},{9,8},{10,11... | collective-permute-start | bytes 98312 | tf_op jit(solution)/shard_map/ppermute | solution.py:408
  19.9 1.7 %collective-permute-start.3 = (f32[4,16,128]{2,1,0:T(8,128)S(1)}, f32[4,16,128]{2,1,0:T(8,128)S(1)}, u32[]{:S(2)}, u32[]{:S(2)}) collective-permute-start(f32[4,16,128]{2,1,0:T(8,128)S(1)} %get-tuple-element.9), channel_id=1, source_target_pairs={{0,32},{32,0},{64,96},{96,64},{1,33},{33,1},{65,97},{97,65},{2,34}... | collective-permute-start | bytes 98312 | tf_op jit(solution)/shard_map/ppermute | solution.py:408
  21.6 0.0 copy-done.1
  21.6 0.0 copy-done.2
  21.6 0.0 copy-done.3
  21.6 2.2 %shard_map.86.new_ref = f32[4,8,16,512]{3,2,1,0:T(8,128)S(1)} custom-call(s32[1,128]{1,0:T(1,128)S(1)} %bitcast.2, f32[1,128]{1,0:T(1,128)S(1)} %bitcast.3, f32[4,8,4,4,512]{4,3,2,1,0:T(4,128)S(1)} %copy-done, f32[64,128]{1,0:T(8,128)S(1)} %copy-done.3), custom_call_target="tpu_custom_call" | custom-call | flops 4000000000 | bytes 4000000 | tf_op jit(solution)/shard_map/pallas_call | solution.py:442
  23.9 0.0 copy-done.4
  23.9 0.1 copy.9.arrival_ref
  24.0 2.0 %collective-permute-done.cross_two = f32[4,4,512]{2,1,0:T(4,128)S(1)} collective-permute-done((f32[4,4,512]{2,1,0:T(4,128)S(1)}, f32[4,4,512]{2,1,0:T(4,128)S(1)}, u32[]{:S(2)}, u32[]{:S(2)}) %collective-permute-start) | collective-permute-done | bytes 32800 | tf_op jit(solution)/shard_map/ppermute | solution.py:408
  26.0 0.0 collective-permute-done.1.along_two
  26.0 0.0 collective-permute-done.2.cross_one
  26.0 0.0 collective-permute-done.3.along_one
  26.0 0.0 all-to-all-done.received_ref
  26.0 2.0 %shard_map.89 = (f32[4,8,4,4,512]{4,3,2,1,0:T(4,128)}, f32[8,4,4,512]{3,2,1,0:T(4,128)}) custom-call(s32[8,4]{1,0:T(8,128)S(1)} %copy.9.arrival_ref, f32[4,8,4,4,512]{4,3,2,1,0:T(4,128)S(1)} %copy-done, f32[4,8,16,512]{3,2,1,0:T(8,128)S(1)} %shard_map.86.new_ref, f32[4,4,512]{2,1,0:T(4,128)S(1)} %collective-permute-done.cross_two, ...), custom_call_target="tpu_custom_call" | custom-call | flops 10000000 | bytes 4000000 | tf_op jit(solution)/shard_map/pallas_call | solution.py:462
  (1 shorter events, 0.0 us)
Async XLA Ops:
  3.7 11.7 %copy-start = (f32[4,8,4,4,512]{4,3,2,1,0:T(4,128)S(1)}, f32[4,8,4,4,512]{4,3,2,1,0:T(4,128)}, u32[]{:S(2)}) copy-start(f32[4,8,4,4,512]{4,3,2,1,0:T(4,128)} %adj_ref.5) | copy-start | bytes 3145732
  3.7 17.9 %copy-start.1 = (s32[128]{0:T(128)S(1)}, s32[128]{0:T(128)}, u32[]{:S(2)}) copy-start(s32[128]{0:T(128)} %param.11) | copy-start | bytes 1540
  3.7 17.9 %copy-start.2 = (f32[128]{0:T(128)S(1)}, f32[128]{0:T(128)}, u32[]{:S(2)}) copy-start(f32[128]{0:T(128)} %param.12) | copy-start | bytes 1540
  3.7 17.9 %copy-start.3 = (f32[64,128]{1,0:T(8,128)S(1)}, f32[64,128]{1,0:T(8,128)}, u32[]{:S(2)}) copy-start(f32[64,128]{1,0:T(8,128)} %constant.2.clone.rows_ref.rows_hbm) | copy-start | bytes 98308
  3.7 22.3 %all-to-all-start = ((f32[32,8,512]{2,1,0:T(8,128)}), f32[32,8,512]{2,1,0:T(8,128)S(1)}, u32[]{:S(2)}, u32[]{:S(2)}) async-start(f32[32,8,512]{2,1,0:T(8,128)} %shard_map.88), calls=%async_computation | async-start | bytes 1048576 | tf_op jit(solution)/shard_map/all_to_all | solution.py:432
  15.7 10.3 %collective-permute-start = (f32[4,4,512]{2,1,0:T(4,128)S(1)}, f32[4,4,512]{2,1,0:T(4,128)S(1)}, u32[]{:S(2)}, u32[]{:S(2)}) collective-permute-start(f32[4,4,512]{2,1,0:T(4,128)S(1)} %get-tuple-element.6), channel_id=1, source_target_pairs={{1,2},{2,1},{3,4},{4,3},{5,6},{6,5},{7,8},{8,7},{9,10},{10,9},{11,... | collective-permute-start | bytes 98312 | tf_op jit(solution)/shard_map/ppermute | solution.py:408
  18.8 7.2 %collective-permute-start.1 = (f32[4,16,128]{2,1,0:T(8,128)S(1)}, f32[4,16,128]{2,1,0:T(8,128)S(1)}, u32[]{:S(2)}, u32[]{:S(2)}) collective-permute-start(f32[4,16,128]{2,1,0:T(8,128)S(1)} %get-tuple-element.7), channel_id=1, source_target_pairs={{32,64},{64,32},{33,65},{65,33},{34,66},{66,34},{35,67},{67,35},{3... | collective-permute-start | bytes 98312 | tf_op jit(solution)/shard_map/ppermute | solution.py:408
  19.5 6.5 %collective-permute-start.2 = (f32[4,4,512]{2,1,0:T(4,128)S(1)}, f32[4,4,512]{2,1,0:T(4,128)S(1)}, u32[]{:S(2)}, u32[]{:S(2)}) collective-permute-start(f32[4,4,512]{2,1,0:T(4,128)S(1)} %get-tuple-element.8), channel_id=1, source_target_pairs={{0,1},{1,0},{2,3},{3,2},{4,5},{5,4},{6,7},{7,6},{8,9},{9,8},{10,11... | collective-permute-start | bytes 98312 | tf_op jit(solution)/shard_map/ppermute | solution.py:408
  19.9 6.1 %collective-permute-start.3 = (f32[4,16,128]{2,1,0:T(8,128)S(1)}, f32[4,16,128]{2,1,0:T(8,128)S(1)}, u32[]{:S(2)}, u32[]{:S(2)}) collective-permute-start(f32[4,16,128]{2,1,0:T(8,128)S(1)} %get-tuple-element.9), channel_id=1, source_target_pairs={{0,32},{32,0},{64,96},{96,64},{1,33},{33,1},{65,97},{97,65},{2,34}... | collective-permute-start | bytes 98312 | tf_op jit(solution)/shard_map/ppermute | solution.py:408
  21.6 2.2 %copy-start.4 = (s32[8,4]{0,1:T(4,128)S(1)}, s32[8,4]{0,1:T(4,128)}, u32[]{:S(2)}) copy-start(s32[8,4]{0,1:T(4,128)} %param.10) | copy-start | bytes 388
